TPU v7x, 32 devices: a whole 2x2x4 slice. The times are simulated.
32 devices in a mesh: view: 4 (over x, core), slab: 8 (over z, y).
Axes of the slice: x: 2, y: 2, z: 4, core: 2. Of those that a mesh axis runs over, the one named last changes fastest.
Arguments:
- atten: float32 [16, 350, 350], P('slab'), may hold values from 0.0005 to 0.008
- view_segment: int32 [8], P('view'), may hold values from 0 to 3
- efficiency: float32 [8, 376, 350], P('view'), may hold values from 0.5 to 2
- live_mask: int32 [8, 376, 350], P('view'), may hold values 0 or 1
Outputs:
- sensitivity: float32 [16, 350, 350], P('slab')
All inputs are finite; a program needn't handle non-finite values. No bound on the sum of `live_mask` on one device may be relied on, other than what follows from the above.
Results may differ from a plain program's by a relative error of at most 0.0003.
Values sent between devices are 32-bit elements; how exact they have to be, the bound alone decides.
A program may use at most 64 MiB of HBM per device.

v0:
```python
import math

import jax
import jax.numpy as jnp
from jax import lax
from jax.sharding import PartitionSpec as P

NSEG = 4


highest = lax.Precision.HIGHEST


def geometry(segment):
    angle = (45.0 + 12.0 * segment.astype(jnp.float32) / (NSEG - 1)) * (math.pi / 180.0)
    slope = jnp.cos(angle) / jnp.sin(angle)
    return (slope, jnp.sqrt(1.0 + slope * slope))


def on_device(atten, view_segment, efficiency, live_mask):
    depth = atten.shape[0]
    cells = atten.shape[1]
    local_views = efficiency.shape[0]
    rows_all = efficiency.shape[1]
    slabs = lax.axis_size("slab")
    total_depth = float(depth * slabs)
    window = cells + depth + 4
    first_slice = (lax.axis_index("slab") * depth).astype(jnp.float32)
    first_view = lax.axis_index("view") * local_views
    plane_iota = lax.broadcasted_iota(jnp.float32, (window, depth, cells), 2)
    row_iota = lax.broadcasted_iota(jnp.float32, (window, depth, cells), 0)
    slice_iota = lax.broadcasted_iota(jnp.float32, (window, depth, cells), 1)
    anchor = jnp.zeros((), jnp.int32)
    partials = []
    shears = []
    starts = []
    lengths = []
    flips = []
    for view in range(local_views):
        slope, length = geometry(view_segment[view])
        flipped = (first_view + view) % 2 == 1
        source = jnp.where(flipped, jnp.swapaxes(atten, 1, 2), atten)
        start = jnp.floor(total_depth + 1.0 - slope * (first_slice + depth - 0.5)).astype(jnp.int32)
        centre = (
            start.astype(jnp.float32)
            + row_iota
            + slope * (first_slice + slice_iota + 0.5)
            - total_depth
            - 2.0
        )
        shear = jnp.maximum(0.0, 1.0 - jnp.abs(plane_iota - centre)).reshape(window, depth * cells)
        ray_window = jnp.dot(
            shear,
            source.reshape(depth * cells, cells),
            precision=highest,
            preferred_element_type=jnp.float32,
        )
        partial_value = lax.dynamic_update_slice(
            jnp.zeros((rows_all, cells), jnp.float32), ray_window, (start, anchor)
        )
        partials.append(partial_value)
        shears.append(shear)
        starts.append(start)
        lengths.append(length)
        flips.append(flipped)
    partial_all = jnp.stack(partials)
    totals = lax.psum(partial_all, "slab")
    sens_part = jnp.zeros((depth, cells, cells), jnp.float32)
    for view in range(local_views):
        start = starts[view]
        line = lengths[view] * lax.dynamic_slice(totals[view], (start, anchor), (window, cells))
        gain = lax.dynamic_slice(efficiency[view], (start, anchor), (window, cells))
        alive = lax.dynamic_slice(live_mask[view], (start, anchor), (window, cells)).astype(
            jnp.float32
        )
        weight_win = gain * alive * jnp.exp(-line)
        spread = lax.dot_general(
            shears[view],
            weight_win,
            (((0,), (0,)), ((), ())),
            precision=highest,
            preferred_element_type=jnp.float32,
        )
        spread = lengths[view] * spread.reshape(depth, cells, cells)
        sens_part = sens_part + jnp.where(flips[view], jnp.swapaxes(spread, 1, 2), spread)
    return lax.psum(sens_part, "view")


def solution(mesh):
    in_specs = (P("slab", None, None), P("view"), P("view", None, None), P("view", None, None))
    out_specs = P("slab", None, None)
    return jax.shard_map(
        on_device, mesh=mesh, in_specs=in_specs, out_specs=out_specs, check_vma=False
    )
```

profile of v0, /device:TPU:0, one launch (start us, length us, event | category | flops | bytes accessed | tf_op | source)
XLA Modules:
  0.0 163.6 jit_solution(6690808495699050831)
XLA Ops:
  6.5 0.0 all-reduce.3.cloned.1.call-start
  6.5 1.3 fusion.94
  9.6 0.0 copy-start
  9.6 2.5 %copy.17 = f32[2,350,350]{1,2,0:T(8,128)S(1)} copy(f32[2,350,350]{2,0,1:T(2,128)} %param.4) | data formatting | bytes 1960000 | tf_op args[0]
  12.2 0.0 copy-done
  12.2 2.5 %convolution_bitcast_fusion = f32[1,356,350]{1,2,0:T(8,128)S(1)} fusion(f32[2,350,350]{1,2,0:T(8,128)S(1)} %copy.17, f32[2,350,350]{2,0,1:T(2,128)S(1)} %copy-done, f32[2]{0:T(128)S(1)} %get-tuple-element.15, f32[356]{0:T(512)S(1)} %iota_add_fusion, pred[]{:T(512)S(6)} %eq.10), kind=kOutput, calls=%fused_computation.2 | convolution fusion | flops 1048380160 | bytes 2459833 | tf_op jit(solution)/shard_map/dot_general | solution.py:52
  14.7 3.0 %dynamic_update_slice.9 = f32[1,376,350]{1,2,0:T(8,128)S(1)} dynamic-update-slice(f32[1,376,350]{1,2,0:T(8,128)S(1)} %stack.11.clone, f32[1,356,350]{1,2,0:T(8,128)S(1)} %convolution_bitcast_fusion, s32[]{:T(128)} %constant.67.clone.1, s32[]{:T(128)S(6)} %select_n.52, s32[]{:T(128)} %constant.67.clone.1) | dynamic-update-slice | bytes 996804 | tf_op jit(solution)/shard_map/dynamic_update_slice | solution.py:58
  17.7 2.5 %convolution_bitcast_fusion.1 = f32[1,356,350]{1,2,0:T(8,128)S(1)} fusion(f32[2,350,350]{1,2,0:T(8,128)S(1)} %copy.17, f32[2,350,350]{2,0,1:T(2,128)S(1)} %copy-done, f32[2]{0:T(128)S(1)} %get-tuple-element.16, f32[356]{0:T(512)S(1)} %iota_add_fusion.1, pred[]{:T(512)S(6)} %eq.9), kind=kOutput, calls=%fused_computation.3 | convolution fusion | flops 1048380160 | bytes 2459833 | tf_op jit(solution)/shard_map/dot_general | solution.py:52
  20.2 3.0 %dynamic_update_slice.8 = f32[1,376,350]{1,2,0:T(8,128)S(1)} dynamic-update-slice(f32[1,376,350]{1,2,0:T(8,128)S(1)} %stack.11.clone.1, f32[1,356,350]{1,2,0:T(8,128)S(1)} %convolution_bitcast_fusion.1, s32[]{:T(128)} %constant.67.clone.1, s32[]{:T(128)S(6)} %select_n.47, s32[]{:T(128)} %constant.67.clone.1) | dynamic-update-slice | bytes 996804 | tf_op jit(solution)/shard_map/dynamic_update_slice | solution.py:58
  23.2 1.1 pad_maximum_fusion
  24.3 0.0 copy-start.1
  24.3 0.0 all-reduce.3.cloned.1.call-update
  24.3 0.2 all-reduce.5.cloned.1.call-start
  24.6 0.9 copy-done.1
  25.5 0.8 fusion.92
  26.4 0.0 copy-start.2
  26.4 3.1 %constant_dynamic-slice_fusion.1 = (f32[1,356,350]{1,0,2:T(1,128)S(1)}, f32[1,356,350]{1,0,2:T(1,128)}) fusion(f32[1,376,350]{1,0,2:T(1,128)S(1)} %get-tuple-element.7, s32[]{:T(128)S(6)} %select_n.52, f32[1,376,350]{1,0,2:T(1,128)S(1)} %get-tuple-element.8, s32[]{:T(128)S(6)} %select_n.47), kind=kLoop, calls=%fused_computation.87 | loop fusion | bytes 1993608 | tf_op jit(solution)/shard_map/dynamic_slice | solution.py:72
  29.5 0.0 copy-done.2
  29.5 0.8 fusion.93
  30.3 3.1 %constant_dynamic-slice_fusion = (s32[1,356,350]{1,0,2:T(1,128)S(1)}, s32[1,356,350]{1,0,2:T(1,128)}) fusion(s32[1,376,350]{1,0,2:T(1,128)S(1)} %get-tuple-element.9, s32[]{:T(128)S(6)} %select_n.52, s32[1,376,350]{1,0,2:T(1,128)S(1)} %get-tuple-element.10, s32[]{:T(128)S(6)} %select_n.47), kind=kLoop, calls=%fused_computation.86 | loop fusion | bytes 1993608 | tf_op jit(solution)/shard_map/dynamic_slice | solution.py:73
  33.4 72.1 %all-reduce.3.cloned.1.call-done = f32[2,376,350]{1,2,0:T(8,128)} async-done(((f32[2,376,350]{1,2,0:T(8,128)}), f32[2,376,350]{1,2,0:T(8,128)}) %all-reduce.3.cloned.1.call-update) | async-done | bytes 1052816 | tf_op jit(solution)/shard_map/psum | solution.py:67
  105.5 2.1 %fusion.91 = (f32[1,376,350]{1,2,0:T(8,128)S(1)}, f32[1,376,350]{1,2,0:T(8,128)}) fusion(f32[2,376,350]{1,2,0:T(8,128)} %all-reduce.3.cloned.1.call-done), kind=kLoop, calls=%fused_computation.106 | loop fusion | bytes 2105600 | tf_op jit(solution)/shard_map/slice | solution.py:71
  107.5 2.5 %convolution_multiply_fusion = f32[2,350,350]{2,1,0:T(8,128)S(1)} fusion(s32[1,356,350]{1,0,2:T(1,128)S(1)} %get-tuple-element.13, f32[1,356,350]{1,0,2:T(1,128)S(1)} %get-tuple-element.17, f32[1,376,350]{1,2,0:T(8,128)S(1)} %get-tuple-element.5, s32[]{:T(128)S(6)} %select_n.52, f32[2]{0:T(128)S(1)} %get-tuple-element.15, f32[356]{0:T(512)S(1)} %iota_add_fusion, ...), kind=kOutput, calls=%fused_computation | convolution fusion | flops 1049003200 | bytes 2506168 | tf_op jit(solution)/shard_map/dot_general | solution.py:77
  110.1 0.4 copy.25
  110.4 3.9 %convolution_multiply_fusion.1 = f32[2,350,350]{2,1,0:T(8,128)S(1)} fusion(s32[1,356,350]{1,0,2:T(1,128)} %get-tuple-element.14, f32[1,356,350]{1,0,2:T(1,128)} %get-tuple-element.18, f32[1,376,350]{1,2,0:T(8,128)} %get-tuple-element.6, s32[]{:T(128)S(6)} %select_n.47, f32[2]{0:T(128)S(1)} %get-tuple-element.16, f32[356]{0:T(512)S(1)} %iota_add_fusion.1, ...), kind=kOutput, calls=%fused_computation.1 | convolution fusion | flops 1049003200 | bytes 2506168 | tf_op jit(solution)/shard_map/dot_general | solution.py:77
  114.3 1.4 copy.22
  115.7 2.4 %fusion.1 = f32[2,350,350]{2,1,0:T(8,128)} fusion(f32[2,350,350]{2,1,0:T(8,128)S(1)} %convolution_multiply_fusion.1, f32[2,350,350]{1,2,0:T(8,128)} %copy.22, f32[2,350,350]{2,1,0:T(8,128)S(1)} %copy.25, f32[2,350,350]{2,1,0:T(8,128)S(1)} %convolution_multiply_fusion, pred[]{:T(512)S(6)} %eq.10, pred[]{:T(512)S(6)} %eq.9), kind=kLoop, calls=%fused_computation.7 | loop fusion | flops 735000 | bytes 4900002 | tf_op jit(solution)/shard_map/add | solution.py:85
  118.1 0.0 all-reduce.5.cloned.1.call-update
  118.1 35.6 %all-reduce.5.cloned.1.call-done = f32[2,350,350]{2,1,0:T(8,128)} async-done(((f32[2,350,350]{2,1,0:T(8,128)}), f32[2,350,350]{2,1,0:T(8,128)}) %all-reduce.5.cloned.1.call-update) | async-done | bytes 980016 | tf_op jit(solution)/shard_map/psum | solution.py:86
  153.7 3.0 %copy.26 = f32[2,350,350]{2,0,1:T(2,128)} copy(f32[2,350,350]{2,1,0:T(8,128)} %all-reduce.5.cloned.1.call-done) | data formatting | bytes 1960000 | tf_op jit(solution)/shard_map/psum | solution.py:86
  (5 shorter events, 0.1 us)
Async XLA Ops:
  6.5 98.9 %all-reduce.3.cloned.1.call-start = ((), (), s32[]{:S(2)}) async-start(), calls=%async_computation | async-start | bytes 2162688 | tf_op jit(solution)/shard_map/psum | solution.py:67
  9.6 2.6 %copy-start = (f32[2,350,350]{2,0,1:T(2,128)S(1)}, f32[2,350,350]{2,0,1:T(2,128)}, u32[]{:S(2)}) copy-start(f32[2,350,350]{2,0,1:T(2,128)} %param.4) | copy-start | bytes 2940004
  24.3 1.2 copy-start.1
  24.3 129.4 %all-reduce.5.cloned.1.call-start = ((), (), s32[]{:S(2)}) async-start(), calls=%async_computation.1 | async-start | bytes 2162688 | tf_op jit(solution)/shard_map/psum | solution.py:86
  26.4 3.1 %copy-start.2 = (s32[2,376,350]{1,0,2:T(2,128)S(1)}, s32[2,376,350]{1,0,2:T(2,128)}, u32[]{:S(2)}) copy-start(s32[2,376,350]{1,0,2:T(2,128)} %param.7) | copy-start | bytes 3158404
Sparse Core Ops, SparseCore 0:
  24.4 80.9 all-reduce.2
  118.3 35.4 all-reduce.4
where the time goes:
time: 164 us
  waiting for transfers between devices  108 us (66%)
  local copies, waits for them, and re-layouts  25.4 us (15%)
  between operations  15.4 us (9%)
  matrix products  11.3 us (7%)
  other arithmetic  3.6 us (2%)
    psum x1, waiting for transfers between devices, on_device(): totals = lax.psum(partial_all, 'slab')  72.1 us
    psum x1, waiting for transfers between devices, on_device(): return lax.psum(sens_part, 'view')  35.6 us
    dot_general x2, matrix products, on_device(): lax.dot_general(shears[view], weight_win, (((0,), (0,)), ((), ())), preci...  6.37 us
    dynamic_update_slice x2, local copies, waits for them, and re-layouts, on_device(): lax.dynamic_update_slice(jnp.zeros((rows_all, cells), jnp.float32), ray_w...  5.91 us
    dot_general x2, matrix products, on_device(): jnp.dot(shear, source.reshape(depth * cells, cells), precision=highest, p...  4.96 us
    unnamed x7, local copies, waits for them, and re-layouts  3.4 us
  transfers between devices with their start and end apart: 2, of which 2 were waited for; matrix products, arithmetic and copies ran while one was open for 5% of the time, Pallas kernels for 0%

commit v1 on v0

v1 whole, which is shorter than its diff:
```python
import functools
import math

import jax
import jax.numpy as jnp
from jax import lax
from jax.experimental import pallas as pl
from jax.experimental.pallas import tpu as pltpu
from jax.sharding import PartitionSpec as P

NSEG = 4
TILE = 8
LANES = 128


def round_up(value, unit):
    return -(-value // unit) * unit


def geometry(segment, total):
    angle = (45.0 + 12.0 * segment / (NSEG - 1)) * (math.pi / 180.0)
    slope = math.cos(angle) / math.sin(angle)
    taps = []
    for z in range(total):
        centre = slope * (z + 0.5) - (total + 2.0)
        lower = math.floor(centre)
        taps.append((-lower, centre - lower))
    return math.sqrt(1.0 + slope * slope), taps


def kernel(dims, seg_ref, att_ref, eff_ref, live_ref, out_ref, nat, src, nat_e, em, slabs_in, em_in, back, image, part, other,
           sem_a, sem_ar, sem_e, sem_er, sem_b, sem_br, sem_c, sem_cr):
    S, D, N, R, L, rows, square, half = dims
    view, slab = lax.axis_index("view"), lax.axis_index("slab")
    side, flip = view // 2, view % 2

    def remote(source, target, send, recv, to_view, to_slab):
        return pltpu.make_async_remote_copy(
            src_ref=source, dst_ref=target, send_sem=send, recv_sem=recv,
            device_id=(to_view, to_slab), device_id_type=pl.DeviceIdType.MESH)

    def block(a_side, a_slab):
        return pl.ds(pl.multiple_of((a_slab * 2 + a_side) * rows, TILE), rows)

    mine = block(side, slab)
    across = 2 * (1 - side) + flip
    beside = 2 * side + 1 - flip
    corner = 2 * (1 - side) + 1 - flip

    barrier = pltpu.get_barrier_semaphore()
    count = 0
    for r in range(S):
        to_slab = lax.rem(slab + r, S)
        for to_view in ((view, across) if r else (across, beside, corner)):
            pl.semaphore_signal(barrier, inc=1, device_id=(to_view, to_slab), device_id_type=pl.DeviceIdType.MESH)
            count += 1

    nat[...] = jnp.zeros_like(nat)
    for d in range(D):
        nat[d, 0:N, 0:N] = att_ref[d]

    @pl.when(flip == 1)
    def _():
        for d in range(D):
            src[d, 0:square, :] = nat[d]

    @pl.when(flip == 0)
    def _():
        for d in range(D):
            for a in range(0, square, LANES):
                for b in range(0, square, LANES):
                    src[d, b:b + LANES, a:a + LANES] = nat[d, a:a + LANES, b:b + LANES].T
            if L > square:
                src[d, 0:square, square:L] = jnp.zeros((square, L - square), jnp.float32)

    pl.semaphore_wait(barrier, count)

    sends = []
    for r in range(1, S):
        to_slab = lax.rem(slab + r, S)
        sends.append(remote(src.at[:, block(side, to_slab), :], slabs_in.at[slab], sem_a.at[r], sem_ar.at[r], view, to_slab))
        sends[-1].start()
    slabs_in[slab] = src[:, mine, :]

    nat_e[...] = jnp.zeros_like(nat_e)
    lane = lax.broadcasted_iota(jnp.int32, (LANES, LANES), 1)
    for v in range(2):
        nat_e[0:R, 0:N] = eff_ref[v] * live_ref[v].astype(jnp.float32)
        for a in range(0, L, LANES):
            for b in range(0, square, LANES):
                turned = nat_e[a:a + LANES, b:b + LANES].T
                if a + LANES == L:
                    turned = jnp.where(lane == LANES - 1, seg_ref[v].astype(jnp.float32), turned)
                em[v, b:b + LANES, a:a + LANES] = turned
    em_sends = []
    for r in range(1, 4):
        to_view = lax.rem(view + r, 4)
        em_sends.append(remote(em.at[to_view % 2, block(to_view // 2, slab), :], em_in.at[view], sem_e.at[r], sem_er.at[r], to_view, slab))
        em_sends[-1].start()
    em_in[view] = em[flip, mine, :]

    for r in range(1, S):
        from_slab = lax.rem(slab + S - r, S)
        remote(src.at[:, mine, :], slabs_in.at[from_slab], sem_a.at[r], sem_ar.at[r], view, from_slab).wait_recv()
    for r in range(1, 4):
        from_view = lax.rem(view + 4 - r, 4)
        remote(em.at[flip, mine, :], em_in.at[from_view], sem_e.at[r], sem_er.at[r], from_view, slab).wait_recv()

    table = [geometry(g, S * D) for g in range(NSEG)]
    for t in range(0, rows, TILE):
        at = slice(t, t + TILE)
        weights = []
        for g in range(NSEG):
            length, taps = table[g]
            sums = {}
            for z, (m, f) in enumerate(taps):
                plane = slabs_in[z // D, z % D, at, :]
                for shift, coef in ((m, 1.0 - f), (m - 1, f)):
                    term = (length * coef) * plane
                    sums[shift] = sums[shift] + term if shift in sums else term
            ray = None
            for shift, value in sums.items():
                moved = pltpu.roll(value, shift, 1)
                ray = moved if ray is None else ray + moved
            gain = jnp.zeros((TILE, L), jnp.float32)
            for j in range(4):
                one = em_in[j, at, :]
                gain = gain + jnp.where(one[:, L - 1:L] == float(g), one, 0.0)
            weights.append(length * (gain * jnp.exp(-ray)))
        moved = {}

        def shifted(g, m):
            if (g, m) not in moved:
                moved[g, m] = pltpu.roll(weights[g], L - m, 1)
            return moved[g, m]

        for z in range(S * D):
            total = None
            for g in range(NSEG):
                m, f = table[g][1][z]
                term = (1.0 - f) * shifted(g, m) + f * shifted(g, m - 1)
                total = term if total is None else total + term
            back[z // D, z % D, at, :] = total

    for r in range(S):
        to_slab = lax.rem(slab + r, S)
        for e in range(2):
            if r or e:
                to_side = (side + e) % 2
                i = 2 * r + e
                sends.append(remote(back.at[to_slab, to_side], image.at[mine, :], sem_b.at[i], sem_br.at[i], 2 * to_side + flip, to_slab))
                sends[-1].start()
    image[mine, :] = back[slab, side]
    for r in range(S):
        from_slab = lax.rem(slab + S - r, S)
        for e in range(2):
            if r or e:
                from_side = (side + e) % 2
                i = 2 * r + e
                remote(back.at[slab, side], image.at[block(from_side, from_slab), :], sem_b.at[i], sem_br.at[i], 2 * from_side + flip, from_slab).wait_recv()

    @pl.when(flip == 1)
    def _():
        part[...] = image[0:square, 0:square]

    @pl.when(flip == 0)
    def _():
        for a in range(0, square, LANES):
            for b in range(0, square, LANES):
                part[b:b + LANES, a:a + LANES] = image[a:a + LANES, b:b + LANES].T

    keep = pl.ds(pl.multiple_of(flip * half, TILE), half)
    give = pl.ds(pl.multiple_of((1 - flip) * half, TILE), half)
    swap = remote(part.at[give, :], other, sem_c.at[0], sem_cr.at[0], beside, slab)
    swap.start()
    swap.wait_recv()
    out_ref[side, keep, :] = part[keep, :] + other[...]
    far = remote(out_ref.at[side, keep, :], out_ref.at[side, keep, :], sem_c.at[1], sem_cr.at[1], across, slab)
    far.start()
    near = remote(out_ref.at[side, keep, :], out_ref.at[side, keep, :], sem_c.at[2], sem_cr.at[2], beside, slab)
    near.start()
    remote(out_ref.at[side, keep, :], out_ref.at[1 - side, keep, :], sem_c.at[1], sem_cr.at[1], across, slab).wait_recv()
    last = remote(out_ref.at[1 - side, keep, :], out_ref.at[1 - side, keep, :], sem_c.at[3], sem_cr.at[3], beside, slab)
    last.start()
    remote(out_ref.at[side, keep, :], out_ref.at[side, give, :], sem_c.at[2], sem_cr.at[2], beside, slab).wait_recv()
    remote(out_ref.at[1 - side, keep, :], out_ref.at[1 - side, give, :], sem_c.at[3], sem_cr.at[3], beside, slab).wait_recv()
    for copy in sends + em_sends + [swap, far, near, last]:
        copy.wait_send()


def on_device(atten, view_segment, efficiency, live_mask):
    S = lax.axis_size("slab")
    D, N = atten.shape[0], atten.shape[1]
    R = efficiency.shape[1]
    assert lax.axis_size("view") == 4 and D == 2 and efficiency.shape[0] == 2
    L = round_up(max(R + 1, N + S * D + 3), LANES)
    square = round_up(N, LANES)
    rows = round_up(-(-N // (2 * S)), TILE)
    total_rows = max(2 * S * rows, square)
    half = round_up(N, 2 * TILE) // 2
    dims = (S, D, N, R, L, rows, square, half)
    f32 = jnp.float32
    dma = pltpu.SemaphoreType.DMA
    vmem = pl.BlockSpec(memory_space=pltpu.VMEM)
    out = pl.pallas_call(
        functools.partial(kernel, dims),
        out_shape=jax.ShapeDtypeStruct((D, 2 * half, square), f32),
        in_specs=[pl.BlockSpec(memory_space=pltpu.SMEM), vmem, vmem, vmem],
        out_specs=vmem,
        scratch_shapes=[
            pltpu.VMEM((D, square, L), f32),
            pltpu.VMEM((D, total_rows, L), f32),
            pltpu.VMEM((L, square), f32),
            pltpu.VMEM((2, total_rows, L), f32),
            pltpu.VMEM((S, D, rows, L), f32),
            pltpu.VMEM((4, rows, L), f32),
            pltpu.VMEM((S, D, rows, L), f32),
            pltpu.VMEM((total_rows, L), f32),
            pltpu.VMEM((square, square), f32),
            pltpu.VMEM((half, square), f32),
            dma((S,)), dma((S,)), dma((4,)), dma((4,)),
            dma((2 * S,)), dma((2 * S,)), dma((4,)), dma((4,)),
        ],
        compiler_params=pltpu.CompilerParams(collective_id=0, has_side_effects=True, vmem_limit_bytes=48 * 2**20),
    )(view_segment, atten, efficiency, live_mask)
    return out[:, :N, :N]


def solution(mesh):
    in_specs = (P("slab", None, None), P("view"), P("view", None, None), P("view", None, None))
    out_specs = P("slab", None, None)
    return jax.shard_map(on_device, mesh=mesh, in_specs=in_specs, out_specs=out_specs, check_vma=False)
```

time: 164 us -> 54.2 us (0.33)
  the two profiles are of different devices: /device:TPU:0 before, /device:TPU:29 now
where the time goes in v1:
time: 54.2 us; the launch traced here: 54 us
  Pallas kernels  47.1 us (87%)
  local copies, waits for them, and re-layouts  6.88 us (13%)
    pallas_call x1, Pallas kernels, on_device(): pl.pallas_call(functools.partial(kernel, dims), out_shape=jax.ShapeDtypeS...  47.1 us
    unnamed x7, local copies, waits for them, and re-layouts  5.07 us
    slice x1, local copies, waits for them, and re-layouts, on_device(): return out[:, :N, :N]  1.81 us

profile of v1, /device:TPU:29, one launch (start us, length us, event | category | flops | bytes accessed | tf_op | source)
XLA Modules:
  0.0 54.0 jit_solution(7028801364214515227)
XLA Ops:
  0.0 0.0 copy-start.1
  0.0 1.4 %copy.5.att_ref = f32[2,350,350]{2,1,0:T(8,128)S(1)} copy(f32[2,350,350]{2,0,1:T(2,128)} %param.4) | data formatting | bytes 1960000 | tf_op args[0]
  1.4 0.2 copy-done.1
  1.6 1.1 %copy.6.eff_ref = f32[2,376,350]{2,1,0:T(8,128)S(1)} copy(f32[2,376,350]{1,0,2:T(2,128)S(1)} %copy-done.1) | data formatting | bytes 2105600 | tf_op args[2]
  2.6 0.0 copy-start
  2.7 2.4 %copy.7.live_ref = s32[2,376,350]{2,1,0:T(8,128)S(1)} copy(s32[2,376,350]{1,0,2:T(2,128)} %param.7) | data formatting | bytes 2105600 | tf_op args[3]
  5.1 0.0 copy-done
  5.1 47.1 %shard_map.46 = f32[2,352,384]{2,1,0:T(8,128)S(1)} custom-call(s32[2]{0:T(128)S(1)} %copy-done, f32[2,350,350]{2,1,0:T(8,128)S(1)} %copy.5.att_ref, f32[2,376,350]{2,1,0:T(8,128)S(1)} %copy.6.eff_ref, s32[2,376,350]{2,1,0:T(8,128)S(1)} %copy.7.live_ref), custom_call_target="tpu_custom_call" | custom-call | tf_op jit(solution)/shard_map/pallas_call | solution.py:205
  52.2 1.8 %copy.8 = f32[2,350,350]{2,0,1:T(2,128)} copy(f32[2,350,350]{2,1,0:T(8,128)S(1)} %bitcast.1) | data formatting | bytes 1960000 | tf_op jit(solution)/shard_map/slice | solution.py:226
Async XLA Ops:
  0.0 1.6 %copy-start.1 = (f32[2,376,350]{1,0,2:T(2,128)S(1)}, f32[2,376,350]{1,0,2:T(2,128)}, u32[]{:S(2)}) copy-start(f32[2,376,350]{1,0,2:T(2,128)} %param.6) | copy-start | bytes 3158404
  2.6 2.5 %copy-start = (s32[2]{0:T(128)S(1)}, s32[2]{0:T(128)}, u32[]{:S(2)}) copy-start(s32[2]{0:T(128)} %seg_ref.1) | copy-start | bytes 28

commit v2 on v1

v2 whole, which is shorter than its diff:
```python
import functools
import math

import jax
import jax.numpy as jnp
from jax import lax
from jax.experimental import pallas as pl
from jax.experimental.pallas import tpu as pltpu
from jax.sharding import PartitionSpec as P

NSEG = 4
TILE = 8
LANES = 128
CHUNK = 16


def round_up(value, unit):
    return -(-value // unit) * unit


def geometry(segment, total):
    angle = (45.0 + 12.0 * segment / (NSEG - 1)) * (math.pi / 180.0)
    slope = math.cos(angle) / math.sin(angle)
    taps = []
    for z in range(total):
        centre = slope * (z + 0.5) - (total + 2.0)
        lower = math.floor(centre)
        taps.append((-lower, centre - lower))
    return math.sqrt(1.0 + slope * slope), taps


def kernel(dims, seg_ref, att_ref, eff_ref, live_ref, out_ref, att_v, eff_v, live_v, nat, src, em, slabs_in, em_in, mid_out, mid_in,
           weights, back, image, part, other, sem_l, sem_a, sem_ar, sem_e, sem_er, sem_m, sem_mr, sem_b, sem_br, sem_c, sem_cr):
    S, D, N, R, L, K, square, half = dims
    U = S // 2
    G = 2 * U
    chunks = -(-N // CHUNK)
    view, slab = lax.axis_index("view"), lax.axis_index("slab")
    side, flip = view // 2, view % 2
    upper, unit = slab // U, slab % U
    f32 = jnp.float32

    def group(a_side, a_unit):
        return a_unit * 2 + a_side

    def rows_of(k, g):
        return pl.ds(pl.multiple_of((k * G + g) * CHUNK, CHUNK), CHUNK)

    def guarded(k, g, act):
        if (k + 1) * G <= chunks:
            act()
        else:
            pl.when(k * G + g < chunks)(act)

    def remote(source, target, send, recv, to_view, to_slab):
        return pltpu.make_async_remote_copy(
            src_ref=source, dst_ref=target, send_sem=send, recv_sem=recv,
            device_id=(to_view, to_slab), device_id_type=pl.DeviceIdType.MESH)

    me = group(side, unit)
    across = 2 * (1 - side) + flip
    beside = 2 * side + 1 - flip
    corner = 2 * (1 - side) + 1 - flip
    partner = (1 - upper) * U + unit

    def in_half(r):
        return upper * U + lax.rem(unit + r, U)

    loads = []
    for d in range(D):
        loads.append(pltpu.make_async_copy(att_ref.at[:, d, :], att_v.at[d], sem_l.at[d]))
    for v in range(2):
        loads.append(pltpu.make_async_copy(eff_ref.at[:, v, :], eff_v.at[v], sem_l.at[D + v]))
        loads.append(pltpu.make_async_copy(live_ref.at[:, v, :], live_v.at[v], sem_l.at[D + 2 + v]))
    for load in loads:
        load.start()

    barrier = pltpu.get_barrier_semaphore()
    greet = [(view, in_half(r)) for r in range(1, U)] + [(across, in_half(r)) for r in range(U)]
    greet += [(beside, slab), (corner, slab), (view, partner)]
    for to in greet:
        pl.semaphore_signal(barrier, inc=1, device_id=to, device_id_type=pl.DeviceIdType.MESH)

    nat[...] = jnp.zeros_like(nat)
    em[...] = jnp.zeros_like(em)
    if chunks * CHUNK < image.shape[0]:
        image[chunks * CHUNK:, :] = jnp.zeros((image.shape[0] - chunks * CHUNK, L), f32)
    for d in range(D):
        loads[d].wait()
        nat[d, 0:N, 0:N] = att_v[d]

    @pl.when(flip == 1)
    def _():
        for c in range(chunks):
            for d in range(D):
                src[c % G, c // G, d] = nat[d, c * CHUNK:(c + 1) * CHUNK, :]

    @pl.when(flip == 0)
    def _():
        for b in range(0, square, LANES):
            for d in range(D):
                for a in range(0, square, LANES):
                    turned = nat[d, a:a + LANES, b:b + LANES].T
                    for i in range(0, LANES, CHUNK):
                        c = (b + i) // CHUNK
                        if c < chunks:
                            src[c % G, c // G, d, :, a:a + LANES] = turned[i:i + CHUNK, :]
        if L > square:
            for c in range(chunks):
                src[c % G, c // G, :, :, square:L] = jnp.zeros((D, CHUNK, L - square), f32)

    pl.semaphore_wait(barrier, len(greet))

    sends = []

    def send(k, g, copy):
        guarded(k, g, copy.start)
        sends.append((k, g, copy))

    for k in range(K):
        for r in range(1, U):
            g = group(side, lax.rem(unit + r, U))
            send(k, g, remote(src.at[g, k], slabs_in.at[k, unit], sem_a.at[k, r], sem_ar.at[k, r], view, in_half(r)))

        def keep_own(k=k):
            slabs_in[k, unit] = src[me, k]

        guarded(k, me, keep_own)

    lane = lax.broadcasted_iota(jnp.int32, (CHUNK, LANES), 1)
    for load in loads[D:]:
        load.wait()
    for v in range(2):
        for c in range(chunks):
            n = min(CHUNK, N - c * CHUNK)
            at = slice(c * CHUNK, c * CHUNK + n)
            em[v, c % G, c // G, 0:n, 0:R] = eff_v[v, at, :] * live_v[v, at, :].astype(f32)
            tail = em[v, c % G, c // G, :, L - LANES:L]
            em[v, c % G, c // G, :, L - LANES:L] = jnp.where(lane == LANES - 1, seg_ref[v].astype(f32), tail)
    em_sends = []
    for r in range(1, 4):
        to_view = lax.rem(view + r, 4)
        em_sends.append(remote(em.at[to_view % 2, group(to_view // 2, unit)], em_in.at[view], sem_e.at[r], sem_er.at[r], to_view, slab))
        em_sends[-1].start()
    em_in[view] = em[flip, me]

    table = [geometry(g, S * D) for g in range(NSEG)]

    def by_half(act):
        pl.when(upper == 0)(functools.partial(act, 0))
        pl.when(upper == 1)(functools.partial(act, 1))

    def project(k):
        for r in range(1, U):
            from_unit = lax.rem(unit + U - r, U)
            remote(src.at[me, k], slabs_in.at[k, from_unit], sem_a.at[k, r], sem_ar.at[k, r], view, upper * U + from_unit).wait_recv()

        def act(h):
            for t in range(0, CHUNK, TILE):
                at = slice(t, t + TILE)
                for g in range(NSEG):
                    length, taps = table[g]
                    sums = {}
                    for n in range(U * D):
                        m, f = taps[h * U * D + n]
                        plane = slabs_in[k, n // D, n % D, at, :]
                        for shift, coef in ((m, 1.0 - f), (m - 1, f)):
                            term = (length * coef) * plane
                            sums[shift] = sums[shift] + term if shift in sums else term
                    ray = None
                    for shift, value in sums.items():
                        moved = pltpu.roll(value, shift, 1)
                        ray = moved if ray is None else ray + moved
                    mid_out[k, g, at, :] = ray

        by_half(act)

    def mid(k):
        return remote(mid_out.at[k], mid_in.at[k], sem_m.at[k], sem_mr.at[k], view, partner)

    def back_project(k):
        mid(k).wait_recv()
        for t in range(0, CHUNK, TILE):
            at = slice(t, t + TILE)
            for g in range(NSEG):
                gain = jnp.zeros((TILE, L), f32)
                for j in range(4):
                    one = em_in[j, k, at, :]
                    gain = gain + jnp.where(one[:, L - 1:L] == float(g), one, 0.0)
                weights[g, at, :] = table[g][0] * (gain * jnp.exp(-(mid_out[k, g, at, :] + mid_in[k, g, at, :])))

        def act(h):
            for t in range(0, CHUNK, TILE):
                at = slice(t, t + TILE)
                moved = {}

                def shifted(g, m):
                    if (g, m) not in moved:
                        moved[g, m] = pltpu.roll(weights[g, at, :], L - m, 1)
                    return moved[g, m]

                for n in range(U * D):
                    total = None
                    for g in range(NSEG):
                        m, f = table[g][1][h * U * D + n]
                        term = (1.0 - f) * shifted(g, m) + f * shifted(g, m - 1)
                        total = term if total is None else total + term
                    back[k, n // D, n % D, at, :] = total

        by_half(act)
        image[rows_of(k, me), :] = back[k, unit, side]

    def finish(k):
        guarded(k, me, functools.partial(back_project, k))
        for r in range(U):
            to_unit = lax.rem(unit + r, U)
            for e in range(2):
                if r or e:
                    to_side = (side + e) % 2
                    i = 2 * r + e
                    send(k, me, remote(back.at[k, to_unit, to_side], image.at[rows_of(k, me), :], sem_b.at[k, i], sem_br.at[k, i],
                                       2 * to_side + flip, in_half(r)))

    for k in range(K):
        guarded(k, me, functools.partial(project, k))
        send(k, me, mid(k))
        if k == 0:
            for r in range(1, 4):
                from_view = lax.rem(view + 4 - r, 4)
                remote(em.at[flip, me], em_in.at[from_view], sem_e.at[r], sem_er.at[r], from_view, slab).wait_recv()
        else:
            finish(k - 1)
    finish(K - 1)

    def arrive(k):
        for r in range(U):
            from_unit = lax.rem(unit + U - r, U)
            for e in range(2):
                if r or e:
                    from_side = (side + e) % 2
                    i = 2 * r + e
                    g = group(from_side, from_unit)
                    copy = remote(back.at[k, unit, side], image.at[rows_of(k, g), :], sem_b.at[k, i], sem_br.at[k, i],
                                  2 * from_side + flip, upper * U + from_unit)
                    guarded(k, g, copy.wait_recv)

    arrived = 0
    for a in range(0, square, LANES):
        while arrived < K and arrived * G * CHUNK < a + LANES:
            arrive(arrived)
            arrived += 1

        @pl.when(flip == 1)
        def _():
            part[a:a + LANES, :] = image[a:a + LANES, 0:square]

        @pl.when(flip == 0)
        def _():
            for b in range(0, square, LANES):
                part[b:b + LANES, a:a + LANES] = image[a:a + LANES, b:b + LANES].T

    keep = pl.ds(pl.multiple_of(flip * half, TILE), half)
    give = pl.ds(pl.multiple_of((1 - flip) * half, TILE), half)
    swap = remote(part.at[give, :], other, sem_c.at[0], sem_cr.at[0], beside, slab)
    swap.start()
    swap.wait_recv()
    out_ref[side, keep, :] = part[keep, :] + other[...]
    far = remote(out_ref.at[side, keep, :], out_ref.at[side, keep, :], sem_c.at[1], sem_cr.at[1], across, slab)
    far.start()
    near = remote(out_ref.at[side, keep, :], out_ref.at[side, keep, :], sem_c.at[2], sem_cr.at[2], beside, slab)
    near.start()
    remote(out_ref.at[side, keep, :], out_ref.at[1 - side, keep, :], sem_c.at[1], sem_cr.at[1], across, slab).wait_recv()
    last = remote(out_ref.at[1 - side, keep, :], out_ref.at[1 - side, keep, :], sem_c.at[3], sem_cr.at[3], beside, slab)
    last.start()
    remote(out_ref.at[side, keep, :], out_ref.at[side, give, :], sem_c.at[2], sem_cr.at[2], beside, slab).wait_recv()
    remote(out_ref.at[1 - side, keep, :], out_ref.at[1 - side, give, :], sem_c.at[3], sem_cr.at[3], beside, slab).wait_recv()
    for k, g, copy in sends:
        guarded(k, g, copy.wait_send)
    for copy in em_sends + [swap, far, near, last]:
        copy.wait_send()


def on_device(atten, view_segment, efficiency, live_mask):
    S = lax.axis_size("slab")
    D, N = atten.shape[0], atten.shape[1]
    R = efficiency.shape[1]
    assert lax.axis_size("view") == 4 and D == 2 and efficiency.shape[0] == 2 and S % 2 == 0
    L = round_up(max(R + 1, N + S * D + 3), LANES)
    square = round_up(N, LANES)
    U = S // 2
    G = 2 * U
    K = -(-N // (G * CHUNK))
    half = round_up(N, 2 * TILE) // 2
    dims = (S, D, N, R, L, K, square, half)
    f32 = jnp.float32
    dma = pltpu.SemaphoreType.DMA
    vmem = pl.BlockSpec(memory_space=pltpu.VMEM)
    anywhere = pl.BlockSpec(memory_space=pl.ANY)
    out = pl.pallas_call(
        functools.partial(kernel, dims),
        out_shape=jax.ShapeDtypeStruct((D, 2 * half, square), f32),
        in_specs=[pl.BlockSpec(memory_space=pltpu.SMEM), anywhere, anywhere, anywhere],
        out_specs=vmem,
        scratch_shapes=[
            pltpu.VMEM((D, N, N), f32),
            pltpu.VMEM((2, N, R), f32),
            pltpu.VMEM((2, N, R), jnp.int32),
            pltpu.VMEM((D, square, L), f32),
            pltpu.VMEM((G, K, D, CHUNK, L), f32),
            pltpu.VMEM((2, G, K, CHUNK, L), f32),
            pltpu.VMEM((K, U, D, CHUNK, L), f32),
            pltpu.VMEM((4, K, CHUNK, L), f32),
            pltpu.VMEM((K, NSEG, CHUNK, L), f32),
            pltpu.VMEM((K, NSEG, CHUNK, L), f32),
            pltpu.VMEM((NSEG, CHUNK, L), f32),
            pltpu.VMEM((K, U, D, CHUNK, L), f32),
            pltpu.VMEM((max(K * G * CHUNK, square), L), f32),
            pltpu.VMEM((square, square), f32),
            pltpu.VMEM((half, square), f32),
            dma((D + 4,)),
            dma((K, U)), dma((K, U)), dma((4,)), dma((4,)),
            dma((K,)), dma((K,)), dma((K, G)), dma((K, G)), dma((4,)), dma((4,)),
        ],
        compiler_params=pltpu.CompilerParams(collective_id=0, has_side_effects=True, vmem_limit_bytes=48 * 2**20),
    )(view_segment, jnp.transpose(atten, (1, 0, 2)), jnp.transpose(efficiency, (2, 0, 1)), jnp.transpose(live_mask, (2, 0, 1)))
    return out[:, :N, :N]


def solution(mesh):
    in_specs = (P("slab", None, None), P("view"), P("view", None, None), P("view", None, None))
    out_specs = P("slab", None, None)
    return jax.shard_map(on_device, mesh=mesh, in_specs=in_specs, out_specs=out_specs, check_vma=False)
```

time: 54.2 us -> 49.7 us (0.917)
  the two profiles are of different devices: /device:TPU:29 before, /device:TPU:0 now
where the time goes in v2:
time: 49.7 us; the launch traced here: 49.5 us
  Pallas kernels  43.3 us (87%)
  local copies, waits for them, and re-layouts  6.16 us (12%)
    pallas_call x1, Pallas kernels, on_device(): pl.pallas_call(functools.partial(kernel, dims), out_shape=jax.ShapeDtypeS...  43.3 us
    unnamed x8, local copies, waits for them, and re-layouts  4.35 us
    slice x1, local copies, waits for them, and re-layouts, on_device(): return out[:, :N, :N]  1.81 us

profile of v2, /device:TPU:0, one launch (start us, length us, event | category | flops | bytes accessed | tf_op | source)
XLA Modules:
  0.0 49.5 jit_solution(14084476294320539054)
XLA Ops:
  0.0 0.0 copy-start
  0.0 1.2 %copy-done = f32[2,350,350]{2,0,1:T(2,128)S(1)} copy-done((f32[2,350,350]{2,0,1:T(2,128)S(1)}, f32[2,350,350]{2,0,1:T(2,128)}, u32[]{:S(2)}) %copy-start) | copy-done | bytes 980024
  1.2 0.0 copy-start.1
  1.2 1.2 %copy-done.1 = f32[2,376,350]{1,0,2:T(2,128)S(1)} copy-done((f32[2,376,350]{1,0,2:T(2,128)S(1)}, f32[2,376,350]{1,0,2:T(2,128)}, u32[]{:S(2)}) %copy-start.1) | copy-done | bytes 1052824
  2.5 0.0 copy-start.2
  2.5 1.2 %copy-done.2 = s32[2,376,350]{1,0,2:T(2,128)S(1)} copy-done((s32[2,376,350]{1,0,2:T(2,128)S(1)}, s32[2,376,350]{1,0,2:T(2,128)}, u32[]{:S(2)}) %copy-start.2) | copy-done | bytes 1052824
  3.7 0.0 copy-start.3
  3.7 0.7 %copy-done.3 = s32[2]{0:T(128)S(1)} copy-done((s32[2]{0:T(128)S(1)}, s32[2]{0:T(128)}, u32[]{:S(2)}) %copy-start.3) | copy-done | bytes 32
  4.4 43.3 %shard_map.46 = f32[2,352,384]{2,1,0:T(8,128)S(1)} custom-call(s32[2]{0:T(128)S(1)} %copy-done.3, f32[350,2,350]{2,1,0:T(2,128)S(1)} %bitcast.5, f32[350,2,376]{2,1,0:T(2,128)S(1)} %bitcast.6, s32[350,2,376]{2,1,0:T(2,128)S(1)} %bitcast.7), custom_call_target="tpu_custom_call" | custom-call | tf_op jit(solution)/shard_map/pallas_call | solution.py:299
  47.7 1.8 %copy.5 = f32[2,350,350]{2,0,1:T(2,128)} copy(f32[2,350,350]{2,1,0:T(8,128)S(1)} %bitcast.4) | data formatting | bytes 1960000 | tf_op jit(solution)/shard_map/slice | solution.py:326
Async XLA Ops:
  0.0 1.2 %copy-start = (f32[2,350,350]{2,0,1:T(2,128)S(1)}, f32[2,350,350]{2,0,1:T(2,128)}, u32[]{:S(2)}) copy-start(f32[2,350,350]{2,0,1:T(2,128)} %param.4) | copy-start | bytes 2940004
  1.2 1.2 %copy-start.1 = (f32[2,376,350]{1,0,2:T(2,128)S(1)}, f32[2,376,350]{1,0,2:T(2,128)}, u32[]{:S(2)}) copy-start(f32[2,376,350]{1,0,2:T(2,128)} %param.6) | copy-start | bytes 3158404
  2.5 1.2 %copy-start.2 = (s32[2,376,350]{1,0,2:T(2,128)S(1)}, s32[2,376,350]{1,0,2:T(2,128)}, u32[]{:S(2)}) copy-start(s32[2,376,350]{1,0,2:T(2,128)} %param.7) | copy-start | bytes 3158404
  3.7 0.7 %copy-start.3 = (s32[2]{0:T(128)S(1)}, s32[2]{0:T(128)}, u32[]{:S(2)}) copy-start(s32[2]{0:T(128)} %seg_ref.1) | copy-start | bytes 28

commit v3 on v2

--- a/solution.py
+++ b/solution.py
@@ -30,7 +30,8 @@
 
 
 def kernel(dims, seg_ref, att_ref, eff_ref, live_ref, out_ref, att_v, eff_v, live_v, nat, src, em, slabs_in, em_in, mid_out, mid_in,
-           weights, back, image, part, other, sem_l, sem_a, sem_ar, sem_e, sem_er, sem_m, sem_mr, sem_b, sem_br, sem_c, sem_cr):
+           weights, back, image, part, other, sem_l, sem_a, sem_ar, sem_e, sem_er, sem_m, sem_mr, sem_b, sem_br,
+           sem_s, sem_sr, sem_f, sem_fr, sem_n, sem_nr, sem_t, sem_tr):
     S, D, N, R, L, K, square, half = dims
     U = S // 2
     G = 2 * U
@@ -82,50 +83,56 @@
         pl.semaphore_signal(barrier, inc=1, device_id=to, device_id_type=pl.DeviceIdType.MESH)
 
     nat[...] = jnp.zeros_like(nat)
+    src[...] = jnp.zeros_like(src)
     em[...] = jnp.zeros_like(em)
     if chunks * CHUNK < image.shape[0]:
         image[chunks * CHUNK:, :] = jnp.zeros((image.shape[0] - chunks * CHUNK, L), f32)
     for d in range(D):
         loads[d].wait()
-        nat[d, 0:N, 0:N] = att_v[d]
-
-    @pl.when(flip == 1)
-    def _():
-        for c in range(chunks):
-            for d in range(D):
-                src[c % G, c // G, d] = nat[d, c * CHUNK:(c + 1) * CHUNK, :]
 
     @pl.when(flip == 0)
     def _():
-        for b in range(0, square, LANES):
+        for d in range(D):
+            nat[d, 0:N, 0:N] = att_v[d]
+
+    pl.semaphore_wait(barrier, len(greet))
+
+    sends = []
+
+    def send(k, g, copy):
+        guarded(k, g, copy.start)
+        sends.append((k, g, copy))
+
+    started = 0
+    for b in range(0, square, LANES):
+        inside = range(b // CHUNK, min((b + LANES) // CHUNK, chunks))
+
+        @pl.when(flip == 1)
+        def _():
+            for c in inside:
+                n = min(CHUNK, N - c * CHUNK)
+                for d in range(D):
+                    src[c % G, c // G, d, 0:n, 0:N] = att_v[d, c * CHUNK:c * CHUNK + n, :]
+
+        @pl.when(flip == 0)
+        def _():
             for d in range(D):
                 for a in range(0, square, LANES):
                     turned = nat[d, a:a + LANES, b:b + LANES].T
-                    for i in range(0, LANES, CHUNK):
-                        c = (b + i) // CHUNK
-                        if c < chunks:
-                            src[c % G, c // G, d, :, a:a + LANES] = turned[i:i + CHUNK, :]
-        if L > square:
-            for c in range(chunks):
-                src[c % G, c // G, :, :, square:L] = jnp.zeros((D, CHUNK, L - square), f32)
-
-    pl.semaphore_wait(barrier, len(greet))
-
-    sends = []
-
-    def send(k, g, copy):
-        guarded(k, g, copy.start)
-        sends.append((k, g, copy))
-
-    for k in range(K):
-        for r in range(1, U):
-            g = group(side, lax.rem(unit + r, U))
-            send(k, g, remote(src.at[g, k], slabs_in.at[k, unit], sem_a.at[k, r], sem_ar.at[k, r], view, in_half(r)))
-
-        def keep_own(k=k):
-            slabs_in[k, unit] = src[me, k]
-
-        guarded(k, me, keep_own)
+                    for c in inside:
+                        src[c % G, c // G, d, :, a:a + LANES] = turned[c * CHUNK - b:(c + 1) * CHUNK - b, :]
+
+        while started < K and ((started + 1) * G * CHUNK <= b + LANES or b + LANES == square):
+            k = started
+            for r in range(1, U):
+                g = group(side, lax.rem(unit + r, U))
+                send(k, g, remote(src.at[g, k], slabs_in.at[k, unit], sem_a.at[k, r], sem_ar.at[k, r], view, in_half(r)))
+
+            def keep_own(k=k):
+                slabs_in[k, unit] = src[me, k]
+
+            guarded(k, me, keep_own)
+            started += 1
 
     lane = lax.broadcasted_iota(jnp.int32, (CHUNK, LANES), 1)
     for load in loads[D:]:
@@ -221,17 +228,6 @@
                     send(k, me, remote(back.at[k, to_unit, to_side], image.at[rows_of(k, me), :], sem_b.at[k, i], sem_br.at[k, i],
                                        2 * to_side + flip, in_half(r)))
 
-    for k in range(K):
-        guarded(k, me, functools.partial(project, k))
-        send(k, me, mid(k))
-        if k == 0:
-            for r in range(1, 4):
-                from_view = lax.rem(view + 4 - r, 4)
-                remote(em.at[flip, me], em_in.at[from_view], sem_e.at[r], sem_er.at[r], from_view, slab).wait_recv()
-        else:
-            finish(k - 1)
-    finish(K - 1)
-
     def arrive(k):
         for r in range(U):
             from_unit = lax.rem(unit + U - r, U)
@@ -244,39 +240,95 @@
                                   2 * from_side + flip, upper * U + from_unit)
                     guarded(k, g, copy.wait_recv)
 
-    arrived = 0
-    for a in range(0, square, LANES):
-        while arrived < K and arrived * G * CHUNK < a + LANES:
-            arrive(arrived)
-            arrived += 1
-
-        @pl.when(flip == 1)
-        def _():
-            part[a:a + LANES, :] = image[a:a + LANES, 0:square]
-
-        @pl.when(flip == 0)
-        def _():
+    bands = square // LANES
+    split = square - LANES
+    regions = (
+        ((0, half, 0, split, 0), (0, half, split, square, 1)),
+        ((half, split, 0, split, 0), (half, split, split, square, 1), (split, 2 * half, 0, square, 1)),
+    )
+    shared = [min((a + 1) * LANES, half) - a * LANES for a in range(bands) if a * LANES < half]
+
+    def swap(f, a):
+        if f == 0:
+            lanes = slice(a * LANES, (a + 1) * LANES)
+            return remote(part.at[half:2 * half, lanes], other.at[:, lanes], sem_s.at[a], sem_sr.at[a], beside, slab)
+        at = slice(a * LANES, a * LANES + shared[a])
+        return remote(image.at[at, 0:square], other.at[at, :], sem_s.at[a], sem_sr.at[a], beside, slab)
+
+    def spread(f, i, a_side, sems, to_view):
+        r0, r1, l0, l1, _ = regions[f][i]
+        place = out_ref.at[a_side, r0:r1, l0:l1]
+        return remote(place, place, sems[0].at[i], sems[1].at[i], to_view, slab)
+
+    far_sems, near_sems, last_sems = (sem_f, sem_fr), (sem_n, sem_nr), (sem_t, sem_tr)
+
+    def band(f, a):
+        if f == 0:
             for b in range(0, square, LANES):
-                part[b:b + LANES, a:a + LANES] = image[a:a + LANES, b:b + LANES].T
-
-    keep = pl.ds(pl.multiple_of(flip * half, TILE), half)
-    give = pl.ds(pl.multiple_of((1 - flip) * half, TILE), half)
-    swap = remote(part.at[give, :], other, sem_c.at[0], sem_cr.at[0], beside, slab)
-    swap.start()
-    swap.wait_recv()
-    out_ref[side, keep, :] = part[keep, :] + other[...]
-    far = remote(out_ref.at[side, keep, :], out_ref.at[side, keep, :], sem_c.at[1], sem_cr.at[1], across, slab)
-    far.start()
-    near = remote(out_ref.at[side, keep, :], out_ref.at[side, keep, :], sem_c.at[2], sem_cr.at[2], beside, slab)
-    near.start()
-    remote(out_ref.at[side, keep, :], out_ref.at[1 - side, keep, :], sem_c.at[1], sem_cr.at[1], across, slab).wait_recv()
-    last = remote(out_ref.at[1 - side, keep, :], out_ref.at[1 - side, keep, :], sem_c.at[3], sem_cr.at[3], beside, slab)
-    last.start()
-    remote(out_ref.at[side, keep, :], out_ref.at[side, give, :], sem_c.at[2], sem_cr.at[2], beside, slab).wait_recv()
-    remote(out_ref.at[1 - side, keep, :], out_ref.at[1 - side, give, :], sem_c.at[3], sem_cr.at[3], beside, slab).wait_recv()
+                part[b:b + LANES, a * LANES:(a + 1) * LANES] = image[a * LANES:(a + 1) * LANES, b:b + LANES].T
+            swap(0, a).start()
+        elif a < len(shared):
+            swap(1, a).start()
+        if a < bands - 2:
+            return
+        stage = a - (bands - 2)
+        if f == 1:
+            for n in range(bands - 1) if stage == 0 else (bands - 1,):
+                swap(0, n).wait_recv()
+        elif stage == 0:
+            for n in range(len(shared)):
+                swap(1, n).wait_recv()
+        for i, (r0, r1, l0, l1, when) in enumerate(regions[f]):
+            if when == stage:
+                own = part if f == 0 else image
+                out_ref[side, r0:r1, l0:l1] = own[r0:r1, l0:l1] + other[r0 - f * half:r1 - f * half, l0:l1]
+                spread(f, i, side, far_sems, across).start()
+                spread(f, i, side, near_sems, beside).start()
+
+    def settle(f):
+        for i in range(len(regions[f])):
+            spread(f, i, 1 - side, far_sems, across).wait_recv()
+            spread(f, i, 1 - side, last_sems, beside).start()
+        for i in range(len(regions[1 - f])):
+            spread(1 - f, i, side, near_sems, beside).wait_recv()
+        for i in range(len(regions[1 - f])):
+            spread(1 - f, i, 1 - side, last_sems, beside).wait_recv()
+        for a in range(bands if f == 0 else len(shared)):
+            swap(f, a).wait_send()
+        for i in range(len(regions[f])):
+            spread(f, i, side, far_sems, across).wait_send()
+            spread(f, i, side, near_sems, beside).wait_send()
+            spread(f, i, 1 - side, last_sems, beside).wait_send()
+
+    progress = {"arrived": 0, "band": 0}
+
+    def ready(k):
+        while progress["arrived"] <= k:
+            arrive(progress["arrived"])
+            progress["arrived"] += 1
+        while progress["band"] < bands and (k == K - 1 or (progress["band"] + 1) * LANES <= (k + 1) * G * CHUNK):
+            for f in range(2):
+                pl.when(flip == f)(functools.partial(band, f, progress["band"]))
+            progress["band"] += 1
+
+    for k in range(K):
+        guarded(k, me, functools.partial(project, k))
+        send(k, me, mid(k))
+        if k == 0:
+            for r in range(1, 4):
+                from_view = lax.rem(view + 4 - r, 4)
+                remote(em.at[flip, me], em_in.at[from_view], sem_e.at[r], sem_er.at[r], from_view, slab).wait_recv()
+        else:
+            finish(k - 1)
+    if K > 1:
+        ready(K - 2)
+    finish(K - 1)
+    ready(K - 1)
+    for f in range(2):
+        pl.when(flip == f)(functools.partial(settle, f))
     for k, g, copy in sends:
         guarded(k, g, copy.wait_send)
-    for copy in em_sends + [swap, far, near, last]:
+    for copy in em_sends:
         copy.wait_send()
 
 
@@ -295,11 +347,11 @@
     f32 = jnp.float32
     dma = pltpu.SemaphoreType.DMA
     vmem = pl.BlockSpec(memory_space=pltpu.VMEM)
-    anywhere = pl.BlockSpec(memory_space=pl.ANY)
+    far = pl.BlockSpec(memory_space=pl.ANY)
     out = pl.pallas_call(
         functools.partial(kernel, dims),
         out_shape=jax.ShapeDtypeStruct((D, 2 * half, square), f32),
-        in_specs=[pl.BlockSpec(memory_space=pltpu.SMEM), anywhere, anywhere, anywhere],
+        in_specs=[pl.BlockSpec(memory_space=pltpu.SMEM), far, far, far],
         out_specs=vmem,
         scratch_shapes=[
             pltpu.VMEM((D, N, N), f32),
@@ -319,9 +371,10 @@
             pltpu.VMEM((half, square), f32),
             dma((D + 4,)),
             dma((K, U)), dma((K, U)), dma((4,)), dma((4,)),
-            dma((K,)), dma((K,)), dma((K, G)), dma((K, G)), dma((4,)), dma((4,)),
+            dma((K,)), dma((K,)), dma((K, G)), dma((K, G)),
+            dma((square // LANES,)), dma((square // LANES,)), *[dma((3,))] * 6,
         ],
-        compiler_params=pltpu.CompilerParams(collective_id=0, has_side_effects=True, vmem_limit_bytes=48 * 2**20),
+        compiler_params=pltpu.CompilerParams(collective_id=0, has_side_effects=True, vmem_limit_bytes=63 * 2**20),
     )(view_segment, jnp.transpose(atten, (1, 0, 2)), jnp.transpose(efficiency, (2, 0, 1)), jnp.transpose(live_mask, (2, 0, 1)))
     return out[:, :N, :N]
 

time: 49.7 us -> 46.3 us (0.932)
  local copies, waits for them, and re-layouts: 6.16 us -> 3.05 us
    unnamed x8 -> x0, local copies, waits for them, and re-layouts: 4.35 us -> none
    slice x1, local copies, waits for them, and re-layouts: 1.81 us -> 3.05 us  [on_device(): return out[:, :N, :N]]
where the time goes in v3:
time: 46.3 us; the launch traced here: 46.1 us
  Pallas kernels  43 us (93%)
  local copies, waits for them, and re-layouts  3.05 us (7%)
    pallas_call x1, Pallas kernels, on_device(): pl.pallas_call(functools.partial(kernel, dims), out_shape=jax.ShapeDtypeS...  43 us
    slice x1, local copies, waits for them, and re-layouts, on_device(): return out[:, :N, :N]  3.05 us

profile of v3, /device:TPU:0, one launch (start us, length us, event | category | flops | bytes accessed | tf_op | source)
XLA Modules:
  0.0 46.1 jit_solution(93142138679000987)
XLA Ops:
  0.0 43.0 %shard_map.46 = f32[2,352,384]{2,1,0:T(8,128)} custom-call(s32[2]{0:T(128)} %seg_ref.1, f32[350,2,350]{2,1,0:T(2,128)} %bitcast.5, f32[350,2,376]{2,1,0:T(2,128)} %bitcast.6, s32[350,2,376]{2,1,0:T(2,128)} %bitcast.7), custom_call_target="tpu_custom_call" | custom-call | tf_op jit(solution)/shard_map/pallas_call | solution.py:351
  43.1 3.0 %copy.5 = f32[2,350,350]{2,0,1:T(2,128)} copy(f32[2,350,350]{2,1,0:T(8,128)} %bitcast.4) | data formatting | bytes 1960000 | tf_op jit(solution)/shard_map/slice | solution.py:379

commit v4 on v3

--- a/solution.py
+++ b/solution.py
@@ -30,8 +30,8 @@
 
 
 def kernel(dims, seg_ref, att_ref, eff_ref, live_ref, out_ref, att_v, eff_v, live_v, nat, src, em, slabs_in, em_in, mid_out, mid_in,
-           weights, back, image, part, other, sem_l, sem_a, sem_ar, sem_e, sem_er, sem_m, sem_mr, sem_b, sem_br,
-           sem_s, sem_sr, sem_f, sem_fr, sem_n, sem_nr, sem_t, sem_tr):
+           weights, back, image, part, other, whole, sem_l, sem_a, sem_ar, sem_e, sem_er, sem_m, sem_mr, sem_b, sem_br,
+           sem_s, sem_sr, sem_f, sem_fr, sem_n, sem_nr, sem_t, sem_tr, sem_w):
     S, D, N, R, L, K, square, half = dims
     U = S // 2
     G = 2 * U
@@ -48,7 +48,7 @@
         return pl.ds(pl.multiple_of((k * G + g) * CHUNK, CHUNK), CHUNK)
 
     def guarded(k, g, act):
-        if (k + 1) * G <= chunks:
+        if isinstance(k, int) and (k + 1) * G <= chunks:
             act()
         else:
             pl.when(k * G + g < chunks)(act)
@@ -70,11 +70,10 @@
     loads = []
     for d in range(D):
         loads.append(pltpu.make_async_copy(att_ref.at[:, d, :], att_v.at[d], sem_l.at[d]))
+        loads[-1].start()
     for v in range(2):
         loads.append(pltpu.make_async_copy(eff_ref.at[:, v, :], eff_v.at[v], sem_l.at[D + v]))
         loads.append(pltpu.make_async_copy(live_ref.at[:, v, :], live_v.at[v], sem_l.at[D + 2 + v]))
-    for load in loads:
-        load.start()
 
     barrier = pltpu.get_barrier_semaphore()
     greet = [(view, in_half(r)) for r in range(1, U)] + [(across, in_half(r)) for r in range(U)]
@@ -82,51 +81,60 @@
     for to in greet:
         pl.semaphore_signal(barrier, inc=1, device_id=to, device_id_type=pl.DeviceIdType.MESH)
 
-    nat[...] = jnp.zeros_like(nat)
-    src[...] = jnp.zeros_like(src)
-    em[...] = jnp.zeros_like(em)
+    def zero_rows(i, carry):
+        nat[i // (square // TILE), pl.ds(pl.multiple_of(i % (square // TILE) * TILE, TILE), TILE), :] = jnp.zeros((TILE, L), f32)
+        return carry
+
+    lax.fori_loop(0, D * square // TILE, zero_rows, 0)
+    if L > square:
+        src[:, :, :, :, square:L] = jnp.zeros((*src.shape[:4], L - square), f32)
     if chunks * CHUNK < image.shape[0]:
         image[chunks * CHUNK:, :] = jnp.zeros((image.shape[0] - chunks * CHUNK, L), f32)
     for d in range(D):
         loads[d].wait()
-
-    @pl.when(flip == 0)
-    def _():
-        for d in range(D):
-            nat[d, 0:N, 0:N] = att_v[d]
+    for load in loads[D:]:
+        load.start()
+    for d in range(D):
+        nat[d, 0:N, 0:N] = att_v[d]
 
     pl.semaphore_wait(barrier, len(greet))
 
-    sends = []
-
-    def send(k, g, copy):
-        guarded(k, g, copy.start)
-        sends.append((k, g, copy))
-
+    def outgoing(k, r):
+        to_unit = lax.rem(unit + r, U)
+        g = group(side, to_unit)
+        return g, remote(src.at[g, k], slabs_in.at[k, unit], sem_a.at[k, r], sem_ar.at[k, r], view, upper * U + to_unit)
+
+    per_band = LANES // CHUNK
     started = 0
     for b in range(0, square, LANES):
-        inside = range(b // CHUNK, min((b + LANES) // CHUNK, chunks))
+        first = b // CHUNK
 
         @pl.when(flip == 1)
         def _():
-            for c in inside:
-                n = min(CHUNK, N - c * CHUNK)
-                for d in range(D):
-                    src[c % G, c // G, d, 0:n, 0:N] = att_v[d, c * CHUNK:c * CHUNK + n, :]
+            def act(i, carry):
+                c = first + i
+                src[c % G, c // G] = nat[:, pl.ds(pl.multiple_of(c * CHUNK, CHUNK), CHUNK), :]
+                return carry
+
+            lax.fori_loop(0, per_band, act, 0)
 
         @pl.when(flip == 0)
         def _():
-            for d in range(D):
+            def act(d, carry):
                 for a in range(0, square, LANES):
                     turned = nat[d, a:a + LANES, b:b + LANES].T
-                    for c in inside:
-                        src[c % G, c // G, d, :, a:a + LANES] = turned[c * CHUNK - b:(c + 1) * CHUNK - b, :]
+                    for i in range(per_band):
+                        c = first + i
+                        src[c % G, c // G, d, :, a:a + LANES] = turned[i * CHUNK:(i + 1) * CHUNK, :]
+                return carry
+
+            lax.fori_loop(0, D, act, 0)
 
         while started < K and ((started + 1) * G * CHUNK <= b + LANES or b + LANES == square):
             k = started
             for r in range(1, U):
-                g = group(side, lax.rem(unit + r, U))
-                send(k, g, remote(src.at[g, k], slabs_in.at[k, unit], sem_a.at[k, r], sem_ar.at[k, r], view, in_half(r)))
+                g, copy = outgoing(k, r)
+                guarded(k, g, copy.start)
 
             def keep_own(k=k):
                 slabs_in[k, unit] = src[me, k]
@@ -137,13 +145,30 @@
     lane = lax.broadcasted_iota(jnp.int32, (CHUNK, LANES), 1)
     for load in loads[D:]:
         load.wait()
+    clear = R // LANES * LANES
     for v in range(2):
-        for c in range(chunks):
-            n = min(CHUNK, N - c * CHUNK)
-            at = slice(c * CHUNK, c * CHUNK + n)
-            em[v, c % G, c // G, 0:n, 0:R] = eff_v[v, at, :] * live_v[v, at, :].astype(f32)
-            tail = em[v, c % G, c // G, :, L - LANES:L]
-            em[v, c % G, c // G, :, L - LANES:L] = jnp.where(lane == LANES - 1, seg_ref[v].astype(f32), tail)
+        tail = jnp.where(lane == LANES - 1, seg_ref[v].astype(f32), 0.0)
+
+        def blank(c, v=v, tail=tail):
+            for a in range(clear, L, LANES):
+                em[v, c % G, c // G, :, a:a + LANES] = tail if a + LANES == L else jnp.zeros((CHUNK, LANES), f32)
+
+        def fill(c, carry, v=v, blank=blank):
+            blank(c)
+            at = pl.ds(pl.multiple_of(c * CHUNK, CHUNK), CHUNK)
+            em[v, c % G, c // G, :, 0:R] = eff_v[v, at, :] * live_v[v, at, :].astype(f32)
+            return carry
+
+        lax.fori_loop(0, N // CHUNK, fill, 0)
+        for c in range(N // CHUNK, K * G):
+            n = N - c * CHUNK
+            if n > 0:
+                blank(c)
+                em[v, c % G, c // G, 0:n, 0:R] = eff_v[v, c * CHUNK:N, :] * live_v[v, c * CHUNK:N, :].astype(f32)
+                if n < CHUNK:
+                    em[v, c % G, c // G, n:, :] = jnp.zeros((CHUNK - n, L), f32)
+            else:
+                em[v, c % G, c // G] = jnp.zeros((CHUNK, L), f32)
     em_sends = []
     for r in range(1, 4):
         to_view = lax.rem(view + r, 4)
@@ -153,6 +178,16 @@
 
     table = [geometry(g, S * D) for g in range(NSEG)]
 
+    def tiles(act):
+        def step(t, carry):
+            act(pl.ds(pl.multiple_of(t * TILE, TILE), TILE))
+            return carry
+
+        if CHUNK == TILE:
+            act(slice(0, TILE))
+        else:
+            lax.fori_loop(0, CHUNK // TILE, step, 0)
+
     def by_half(act):
         pl.when(upper == 0)(functools.partial(act, 0))
         pl.when(upper == 1)(functools.partial(act, 1))
@@ -163,8 +198,8 @@
             remote(src.at[me, k], slabs_in.at[k, from_unit], sem_a.at[k, r], sem_ar.at[k, r], view, upper * U + from_unit).wait_recv()
 
         def act(h):
-            for t in range(0, CHUNK, TILE):
-                at = slice(t, t + TILE)
+            @tiles
+            def _(at):
                 for g in range(NSEG):
                     length, taps = table[g]
                     sums = {}
@@ -187,8 +222,8 @@
 
     def back_project(k):
         mid(k).wait_recv()
-        for t in range(0, CHUNK, TILE):
-            at = slice(t, t + TILE)
+        @tiles
+        def _(at):
             for g in range(NSEG):
                 gain = jnp.zeros((TILE, L), f32)
                 for j in range(4):
@@ -197,8 +232,8 @@
                 weights[g, at, :] = table[g][0] * (gain * jnp.exp(-(mid_out[k, g, at, :] + mid_in[k, g, at, :])))
 
         def act(h):
-            for t in range(0, CHUNK, TILE):
-                at = slice(t, t + TILE)
+            @tiles
+            def _(at):
                 moved = {}
 
                 def shifted(g, m):
@@ -217,16 +252,20 @@
         by_half(act)
         image[rows_of(k, me), :] = back[k, unit, side]
 
-    def finish(k):
-        guarded(k, me, functools.partial(back_project, k))
+    def returning(k):
         for r in range(U):
             to_unit = lax.rem(unit + r, U)
             for e in range(2):
                 if r or e:
                     to_side = (side + e) % 2
                     i = 2 * r + e
-                    send(k, me, remote(back.at[k, to_unit, to_side], image.at[rows_of(k, me), :], sem_b.at[k, i], sem_br.at[k, i],
-                                       2 * to_side + flip, in_half(r)))
+                    yield remote(back.at[k, to_unit, to_side], image.at[rows_of(k, me), :], sem_b.at[k, i], sem_br.at[k, i],
+                                 2 * to_side + flip, upper * U + to_unit)
+
+    def finish(k):
+        back_project(k)
+        for copy in returning(k):
+            copy.start()
 
     def arrive(k):
         for r in range(U):
@@ -257,8 +296,12 @@
 
     def spread(f, i, a_side, sems, to_view):
         r0, r1, l0, l1, _ = regions[f][i]
-        place = out_ref.at[a_side, r0:r1, l0:l1]
+        place = whole.at[a_side, r0:r1, l0:l1]
         return remote(place, place, sems[0].at[i], sems[1].at[i], to_view, slab)
+
+    def write(f, i, a_side, n):
+        r0, r1, l0, l1, _ = regions[f][i]
+        return pltpu.make_async_copy(whole.at[a_side, r0:r1, l0:l1], out_ref.at[r0:r1, a_side, l0:l1], sem_w.at[n, i])
 
     far_sems, near_sems, last_sems = (sem_f, sem_fr), (sem_n, sem_nr), (sem_t, sem_tr)
 
@@ -281,18 +324,28 @@
         for i, (r0, r1, l0, l1, when) in enumerate(regions[f]):
             if when == stage:
                 own = part if f == 0 else image
-                out_ref[side, r0:r1, l0:l1] = own[r0:r1, l0:l1] + other[r0 - f * half:r1 - f * half, l0:l1]
+                whole[side, r0:r1, l0:l1] = own[r0:r1, l0:l1] + other[r0 - f * half:r1 - f * half, l0:l1]
                 spread(f, i, side, far_sems, across).start()
                 spread(f, i, side, near_sems, beside).start()
+                write(f, i, side, 0).start()
 
     def settle(f):
         for i in range(len(regions[f])):
             spread(f, i, 1 - side, far_sems, across).wait_recv()
             spread(f, i, 1 - side, last_sems, beside).start()
+            write(f, i, 1 - side, 1).start()
         for i in range(len(regions[1 - f])):
             spread(1 - f, i, side, near_sems, beside).wait_recv()
+            write(1 - f, i, side, 2).start()
         for i in range(len(regions[1 - f])):
             spread(1 - f, i, 1 - side, last_sems, beside).wait_recv()
+            write(1 - f, i, 1 - side, 3).start()
+        for i in range(len(regions[f])):
+            write(f, i, side, 0).wait()
+            write(f, i, 1 - side, 1).wait()
+        for i in range(len(regions[1 - f])):
+            write(1 - f, i, side, 2).wait()
+            write(1 - f, i, 1 - side, 3).wait()
         for a in range(bands if f == 0 else len(shared)):
             swap(f, a).wait_send()
         for i in range(len(regions[f])):
@@ -303,31 +356,59 @@
     progress = {"arrived": 0, "band": 0}
 
     def ready(k):
-        while progress["arrived"] <= k:
-            arrive(progress["arrived"])
-            progress["arrived"] += 1
+        def act(n, carry):
+            arrive(n)
+            return carry
+
+        lax.fori_loop(progress["arrived"], k + 1, act, 0)
+        progress["arrived"] = k + 1
         while progress["band"] < bands and (k == K - 1 or (progress["band"] + 1) * LANES <= (k + 1) * G * CHUNK):
             for f in range(2):
                 pl.when(flip == f)(functools.partial(band, f, progress["band"]))
             progress["band"] += 1
 
-    for k in range(K):
-        guarded(k, me, functools.partial(project, k))
-        send(k, me, mid(k))
-        if k == 0:
+    def step(k, carry):
+        @pl.when((k < K) & (k * G + me < chunks))
+        def _():
+            project(k)
+            mid(k).start()
+
+        @pl.when(k == 0)
+        def _():
             for r in range(1, 4):
                 from_view = lax.rem(view + 4 - r, 4)
                 remote(em.at[flip, me], em_in.at[from_view], sem_e.at[r], sem_er.at[r], from_view, slab).wait_recv()
-        else:
+
+        if K > 1:
+            @pl.when(k == K)
+            def _():
+                ready(K - 2)
+
+        @pl.when((k > 0) & ((k - 1) * G + me < chunks))
+        def _():
             finish(k - 1)
-    if K > 1:
-        ready(K - 2)
-    finish(K - 1)
+
+        return carry
+
+    lax.fori_loop(0, K + 1, step, 0)
     ready(K - 1)
     for f in range(2):
         pl.when(flip == f)(functools.partial(settle, f))
-    for k, g, copy in sends:
-        guarded(k, g, copy.wait_send)
+
+    def drain(k, carry):
+        for r in range(1, U):
+            g, copy = outgoing(k, r)
+            guarded(k, g, copy.wait_send)
+
+        @pl.when(k * G + me < chunks)
+        def _():
+            mid(k).wait_send()
+            for copy in returning(k):
+                copy.wait_send()
+
+        return carry
+
+    lax.fori_loop(0, K, drain, 0)
     for copy in em_sends:
         copy.wait_send()
 
@@ -346,19 +427,18 @@
     dims = (S, D, N, R, L, K, square, half)
     f32 = jnp.float32
     dma = pltpu.SemaphoreType.DMA
-    vmem = pl.BlockSpec(memory_space=pltpu.VMEM)
     far = pl.BlockSpec(memory_space=pl.ANY)
     out = pl.pallas_call(
         functools.partial(kernel, dims),
-        out_shape=jax.ShapeDtypeStruct((D, 2 * half, square), f32),
+        out_shape=jax.ShapeDtypeStruct((2 * half, D, square), f32),
         in_specs=[pl.BlockSpec(memory_space=pltpu.SMEM), far, far, far],
-        out_specs=vmem,
+        out_specs=far,
         scratch_shapes=[
             pltpu.VMEM((D, N, N), f32),
             pltpu.VMEM((2, N, R), f32),
             pltpu.VMEM((2, N, R), jnp.int32),
             pltpu.VMEM((D, square, L), f32),
-            pltpu.VMEM((G, K, D, CHUNK, L), f32),
+            pltpu.VMEM((G, max(K, -(-square // (G * CHUNK))), D, CHUNK, L), f32),
             pltpu.VMEM((2, G, K, CHUNK, L), f32),
             pltpu.VMEM((K, U, D, CHUNK, L), f32),
             pltpu.VMEM((4, K, CHUNK, L), f32),
@@ -369,14 +449,15 @@
             pltpu.VMEM((max(K * G * CHUNK, square), L), f32),
             pltpu.VMEM((square, square), f32),
             pltpu.VMEM((half, square), f32),
+            pltpu.VMEM((D, 2 * half, square), f32),
             dma((D + 4,)),
             dma((K, U)), dma((K, U)), dma((4,)), dma((4,)),
             dma((K,)), dma((K,)), dma((K, G)), dma((K, G)),
-            dma((square // LANES,)), dma((square // LANES,)), *[dma((3,))] * 6,
+            dma((square // LANES,)), dma((square // LANES,)), *[dma((3,))] * 6, dma((4, 3)),
         ],
         compiler_params=pltpu.CompilerParams(collective_id=0, has_side_effects=True, vmem_limit_bytes=63 * 2**20),
     )(view_segment, jnp.transpose(atten, (1, 0, 2)), jnp.transpose(efficiency, (2, 0, 1)), jnp.transpose(live_mask, (2, 0, 1)))
-    return out[:, :N, :N]
+    return jnp.transpose(out[:N, :, :N], (1, 0, 2))
 
 
 def solution(mesh):

time: 46.3 us -> 46.4 us (level)
  Pallas kernels: 43 us -> 43.7 us
  local copies, waits for them, and re-layouts: 3.05 us -> 2.58 us
    slice x1 -> x0, local copies, waits for them, and re-layouts: 3.05 us -> none  [on_device(): return out[:, :N, :N]]
    transpose x0 -> x1, local copies, waits for them, and re-layouts: none -> 2.58 us  [on_device(): return jnp.transpose(out[:N, :, :N], (1, 0, 2))]
    pallas_call x1, Pallas kernels: 43 us -> 43.7 us  [on_device(): pl.pallas_call(functools.partial(kernel, dims), out_shape=jax.ShapeDtypeS...]
where the time goes in v4:
time: 46.4 us; the launch traced here: 46.3 us
  Pallas kernels  43.7 us (94%)
  local copies, waits for them, and re-layouts  2.58 us (6%)
    pallas_call x1, Pallas kernels, on_device(): pl.pallas_call(functools.partial(kernel, dims), out_shape=jax.ShapeDtypeS...  43.7 us
    transpose x1, local copies, waits for them, and re-layouts, on_device(): return jnp.transpose(out[:N, :, :N], (1, 0, 2))  2.58 us

profile of v4, /device:TPU:0, one launch (start us, length us, event | category | flops | bytes accessed | tf_op | source)
XLA Modules:
  0.0 46.3 jit_solution(13541691054894660746)
XLA Ops:
  0.0 43.7 %shard_map.46 = f32[352,2,384]{2,1,0:T(2,128)} custom-call(s32[2]{0:T(128)} %seg_ref.1, f32[350,2,350]{2,1,0:T(2,128)} %bitcast.5, f32[350,2,376]{2,1,0:T(2,128)} %bitcast.6, s32[350,2,376]{2,1,0:T(2,128)} %bitcast.7), custom_call_target="tpu_custom_call" | custom-call | tf_op jit(solution)/shard_map/pallas_call | solution.py:431
  43.7 2.6 %slice_bitcast_fusion = f32[2,350,350]{2,0,1:T(2,128)} fusion(f32[352,2,384]{2,1,0:T(2,128)} %shard_map.46), kind=kLoop, calls=%fused_computation | loop fusion | bytes 1960000 | tf_op jit(solution)/shard_map/transpose | solution.py:460

commit v5 on v4

--- a/solution.py
+++ b/solution.py
@@ -30,7 +30,7 @@
 
 
 def kernel(dims, seg_ref, att_ref, eff_ref, live_ref, out_ref, att_v, eff_v, live_v, nat, src, em, slabs_in, em_in, mid_out, mid_in,
-           weights, back, image, part, other, whole, sem_l, sem_a, sem_ar, sem_e, sem_er, sem_m, sem_mr, sem_b, sem_br,
+           weights, back, image, part, other, whole, sem_l, sem_g, sem_a, sem_ar, sem_e, sem_er, sem_m, sem_mr, sem_b, sem_br,
            sem_s, sem_sr, sem_f, sem_fr, sem_n, sem_nr, sem_t, sem_tr, sem_w):
     S, D, N, R, L, K, square, half = dims
     U = S // 2
@@ -71,9 +71,28 @@
     for d in range(D):
         loads.append(pltpu.make_async_copy(att_ref.at[:, d, :], att_v.at[d], sem_l.at[d]))
         loads[-1].start()
-    for v in range(2):
-        loads.append(pltpu.make_async_copy(eff_ref.at[:, v, :], eff_v.at[v], sem_l.at[D + v]))
-        loads.append(pltpu.make_async_copy(live_ref.at[:, v, :], live_v.at[v], sem_l.at[D + 2 + v]))
+
+    full = N // CHUNK
+
+    def gains(v, a, k, start):
+        at = pl.ds(start, CHUNK)
+        return (pltpu.make_async_copy(eff_ref.at[at, v, :], eff_v.at[v, a, k], sem_g.at[0, v, a, k]),
+                pltpu.make_async_copy(live_ref.at[at, v, :], live_v.at[v, a, k], sem_g.at[1, v, a, k]))
+
+    def load_gains(k, carry):
+        for a in range(2):
+            c = k * G + group(a, unit)
+            for v in range(2):
+                @pl.when(c < full)
+                def _():
+                    for copy in gains(v, a, k, c * CHUNK):
+                        copy.start()
+
+                @pl.when(c >= full)
+                def _():
+                    for copy in gains(v, a, k, N - CHUNK):
+                        copy.start()
+        return carry
 
     barrier = pltpu.get_barrier_semaphore()
     greet = [(view, in_half(r)) for r in range(1, U)] + [(across, in_half(r)) for r in range(U)]
@@ -92,8 +111,7 @@
         image[chunks * CHUNK:, :] = jnp.zeros((image.shape[0] - chunks * CHUNK, L), f32)
     for d in range(D):
         loads[d].wait()
-    for load in loads[D:]:
-        load.start()
+    lax.fori_loop(0, K, load_gains, 0)
     for d in range(D):
         nat[d, 0:N, 0:N] = att_v[d]
 
@@ -143,38 +161,36 @@
             started += 1
 
     lane = lax.broadcasted_iota(jnp.int32, (CHUNK, LANES), 1)
-    for load in loads[D:]:
-        load.wait()
     clear = R // LANES * LANES
-    for v in range(2):
-        tail = jnp.where(lane == LANES - 1, seg_ref[v].astype(f32), 0.0)
-
-        def blank(c, v=v, tail=tail):
-            for a in range(clear, L, LANES):
-                em[v, c % G, c // G, :, a:a + LANES] = tail if a + LANES == L else jnp.zeros((CHUNK, LANES), f32)
-
-        def fill(c, carry, v=v, blank=blank):
-            blank(c)
-            at = pl.ds(pl.multiple_of(c * CHUNK, CHUNK), CHUNK)
-            em[v, c % G, c // G, :, 0:R] = eff_v[v, at, :] * live_v[v, at, :].astype(f32)
-            return carry
-
-        lax.fori_loop(0, N // CHUNK, fill, 0)
-        for c in range(N // CHUNK, K * G):
-            n = N - c * CHUNK
-            if n > 0:
-                blank(c)
-                em[v, c % G, c // G, 0:n, 0:R] = eff_v[v, c * CHUNK:N, :] * live_v[v, c * CHUNK:N, :].astype(f32)
-                if n < CHUNK:
-                    em[v, c % G, c // G, n:, :] = jnp.zeros((CHUNK - n, L), f32)
-            else:
-                em[v, c % G, c // G] = jnp.zeros((CHUNK, L), f32)
+
+    def fill(k, carry):
+        for a in range(2):
+            c = k * G + group(a, unit)
+            for v in range(2):
+                for copy in gains(v, a, k, N - CHUNK):
+                    copy.wait()
+                for b in range(clear, L, LANES):
+                    blank = jnp.where(lane == LANES - 1, seg_ref[v].astype(f32), 0.0) if b + LANES == L else jnp.zeros((CHUNK, LANES), f32)
+                    em[v, a, k, :, b:b + LANES] = blank
+                gain = eff_v[v, a, k] * live_v[v, a, k].astype(f32)
+
+                @pl.when(c < full)
+                def _():
+                    em[v, a, k, :, 0:R] = gain
+
+                if N % CHUNK:
+                    @pl.when(c >= full)
+                    def _():
+                        em[v, a, k, 0:N % CHUNK, 0:R] = gain[CHUNK - N % CHUNK:, :]
+        return carry
+
+    lax.fori_loop(0, K, fill, 0)
     em_sends = []
     for r in range(1, 4):
         to_view = lax.rem(view + r, 4)
-        em_sends.append(remote(em.at[to_view % 2, group(to_view // 2, unit)], em_in.at[view], sem_e.at[r], sem_er.at[r], to_view, slab))
+        em_sends.append(remote(em.at[to_view % 2, to_view // 2], em_in.at[view], sem_e.at[r], sem_er.at[r], to_view, slab))
         em_sends[-1].start()
-    em_in[view] = em[flip, me]
+    em_in[view] = em[flip, side]
 
     table = [geometry(g, S * D) for g in range(NSEG)]
 
@@ -367,30 +383,32 @@
                 pl.when(flip == f)(functools.partial(band, f, progress["band"]))
             progress["band"] += 1
 
-    def step(k, carry):
-        @pl.when((k < K) & (k * G + me < chunks))
+    def first_pass(k, carry):
+        @pl.when(k * G + me < chunks)
         def _():
             project(k)
             mid(k).start()
 
-        @pl.when(k == 0)
-        def _():
-            for r in range(1, 4):
-                from_view = lax.rem(view + 4 - r, 4)
-                remote(em.at[flip, me], em_in.at[from_view], sem_e.at[r], sem_er.at[r], from_view, slab).wait_recv()
-
+        return carry
+
+    lax.fori_loop(0, K, first_pass, 0)
+    for r in range(1, 4):
+        from_view = lax.rem(view + 4 - r, 4)
+        remote(em.at[flip, side], em_in.at[from_view], sem_e.at[r], sem_er.at[r], from_view, slab).wait_recv()
+
+    def second_pass(k, carry):
         if K > 1:
-            @pl.when(k == K)
+            @pl.when(k == K - 1)
             def _():
                 ready(K - 2)
 
-        @pl.when((k > 0) & ((k - 1) * G + me < chunks))
+        @pl.when(k * G + me < chunks)
         def _():
-            finish(k - 1)
-
-        return carry
-
-    lax.fori_loop(0, K + 1, step, 0)
+            finish(k)
+
+        return carry
+
+    lax.fori_loop(0, K, second_pass, 0)
     ready(K - 1)
     for f in range(2):
         pl.when(flip == f)(functools.partial(settle, f))
@@ -435,11 +453,11 @@
         out_specs=far,
         scratch_shapes=[
             pltpu.VMEM((D, N, N), f32),
-            pltpu.VMEM((2, N, R), f32),
-            pltpu.VMEM((2, N, R), jnp.int32),
+            pltpu.VMEM((2, 2, K, CHUNK, R), f32),
+            pltpu.VMEM((2, 2, K, CHUNK, R), jnp.int32),
             pltpu.VMEM((D, square, L), f32),
             pltpu.VMEM((G, max(K, -(-square // (G * CHUNK))), D, CHUNK, L), f32),
-            pltpu.VMEM((2, G, K, CHUNK, L), f32),
+            pltpu.VMEM((2, 2, K, CHUNK, L), f32),
             pltpu.VMEM((K, U, D, CHUNK, L), f32),
             pltpu.VMEM((4, K, CHUNK, L), f32),
             pltpu.VMEM((K, NSEG, CHUNK, L), f32),
@@ -450,7 +468,7 @@
             pltpu.VMEM((square, square), f32),
             pltpu.VMEM((half, square), f32),
             pltpu.VMEM((D, 2 * half, square), f32),
-            dma((D + 4,)),
+            dma((D,)), dma((2, 2, 2, K)),
             dma((K, U)), dma((K, U)), dma((4,)), dma((4,)),
             dma((K,)), dma((K,)), dma((K, G)), dma((K, G)),
             dma((square // LANES,)), dma((square // LANES,)), *[dma((3,))] * 6, dma((4, 3)),

time: 46.4 us -> 47.2 us (1.017)
  Pallas kernels: 43.7 us -> 44.4 us
    pallas_call x1, Pallas kernels: 43.7 us -> 44.4 us  [on_device(): pl.pallas_call(functools.partial(kernel, dims), out_shape=jax.ShapeDtypeS...]
where the time goes in v5:
time: 47.2 us; the launch traced here: 47 us
  Pallas kernels  44.4 us (94%)
  local copies, waits for them, and re-layouts  2.58 us (5%)
    pallas_call x1, Pallas kernels, on_device(): pl.pallas_call(functools.partial(kernel, dims), out_shape=jax.ShapeDtypeS...  44.4 us
    transpose x1, local copies, waits for them, and re-layouts, on_device(): return jnp.transpose(out[:N, :, :N], (1, 0, 2))  2.58 us

profile of v5, /device:TPU:0, one launch (start us, length us, event | category | flops | bytes accessed | tf_op | source)
XLA Modules:
  0.0 47.0 jit_solution(13514596935158346591)
XLA Ops:
  0.0 44.4 %shard_map.46 = f32[352,2,384]{2,1,0:T(2,128)} custom-call(s32[2]{0:T(128)} %seg_ref.1, f32[350,2,350]{2,1,0:T(2,128)} %bitcast.5, f32[350,2,376]{2,1,0:T(2,128)} %bitcast.6, s32[350,2,376]{2,1,0:T(2,128)} %bitcast.7), custom_call_target="tpu_custom_call" | custom-call | tf_op jit(solution)/shard_map/pallas_call | solution.py:449
  44.5 2.6 %slice_bitcast_fusion = f32[2,350,350]{2,0,1:T(2,128)} fusion(f32[352,2,384]{2,1,0:T(2,128)} %shard_map.46), kind=kLoop, calls=%fused_computation | loop fusion | bytes 1960000 | tf_op jit(solution)/shard_map/transpose | solution.py:478

commit v6 on v5

--- a/solution.py
+++ b/solution.py
@@ -11,7 +11,8 @@
 NSEG = 4
 TILE = 8
 LANES = 128
-CHUNK = 16
+CHUNK = 8
+AHEAD = 2
 
 
 def round_up(value, unit):
@@ -383,32 +384,30 @@
                 pl.when(flip == f)(functools.partial(band, f, progress["band"]))
             progress["band"] += 1
 
-    def first_pass(k, carry):
-        @pl.when(k * G + me < chunks)
+    def step(k, carry):
+        @pl.when((k < K) & (k * G + me < chunks))
         def _():
             project(k)
             mid(k).start()
 
-        return carry
-
-    lax.fori_loop(0, K, first_pass, 0)
-    for r in range(1, 4):
-        from_view = lax.rem(view + 4 - r, 4)
-        remote(em.at[flip, side], em_in.at[from_view], sem_e.at[r], sem_er.at[r], from_view, slab).wait_recv()
-
-    def second_pass(k, carry):
+        @pl.when(k == AHEAD)
+        def _():
+            for r in range(1, 4):
+                from_view = lax.rem(view + 4 - r, 4)
+                remote(em.at[flip, side], em_in.at[from_view], sem_e.at[r], sem_er.at[r], from_view, slab).wait_recv()
+
         if K > 1:
-            @pl.when(k == K - 1)
+            @pl.when(k == K - 1 + AHEAD)
             def _():
                 ready(K - 2)
 
-        @pl.when(k * G + me < chunks)
-        def _():
-            finish(k)
+        @pl.when((k >= AHEAD) & ((k - AHEAD) * G + me < chunks))
+        def _():
+            finish(k - AHEAD)
 
         return carry
 
-    lax.fori_loop(0, K, second_pass, 0)
+    lax.fori_loop(0, K + AHEAD, step, 0)
     ready(K - 1)
     for f in range(2):
         pl.when(flip == f)(functools.partial(settle, f))

time: 47.2 us -> 46.7 us (0.989)
    pallas_call x1, Pallas kernels: 44.4 us -> 44 us  [on_device(): pl.pallas_call(functools.partial(kernel, dims), out_shape=jax.ShapeDtypeS...]
where the time goes in v6:
time: 46.7 us; the launch traced here: 46.5 us
  Pallas kernels  44 us (94%)
  local copies, waits for them, and re-layouts  2.58 us (6%)
    pallas_call x1, Pallas kernels, on_device(): pl.pallas_call(functools.partial(kernel, dims), out_shape=jax.ShapeDtypeS...  44 us
    transpose x1, local copies, waits for them, and re-layouts, on_device(): return jnp.transpose(out[:N, :, :N], (1, 0, 2))  2.58 us

profile of v6, /device:TPU:0, one launch (start us, length us, event | category | flops | bytes accessed | tf_op | source)
XLA Modules:
  0.0 46.5 jit_solution(15955953293724863433)
XLA Ops:
  0.0 44.0 %shard_map.46 = f32[352,2,384]{2,1,0:T(2,128)} custom-call(s32[2]{0:T(128)} %seg_ref.1, f32[350,2,350]{2,1,0:T(2,128)} %bitcast.5, f32[350,2,376]{2,1,0:T(2,128)} %bitcast.6, s32[350,2,376]{2,1,0:T(2,128)} %bitcast.7), custom_call_target="tpu_custom_call" | custom-call | tf_op jit(solution)/shard_map/pallas_call | solution.py:448
  44.0 2.6 %slice_bitcast_fusion = f32[2,350,350]{2,0,1:T(2,128)} fusion(f32[352,2,384]{2,1,0:T(2,128)} %shard_map.46), kind=kLoop, calls=%fused_computation | loop fusion | bytes 1960000 | tf_op jit(solution)/shard_map/transpose | solution.py:477

commit v7 on v6

--- a/solution.py
+++ b/solution.py
@@ -112,8 +112,8 @@
         image[chunks * CHUNK:, :] = jnp.zeros((image.shape[0] - chunks * CHUNK, L), f32)
     for d in range(D):
         loads[d].wait()
-    lax.fori_loop(0, K, load_gains, 0)
-    for d in range(D):
+        if d == D - 1:
+            lax.fori_loop(0, K, load_gains, 0)
         nat[d, 0:N, 0:N] = att_v[d]
 
     pl.semaphore_wait(barrier, len(greet))
@@ -354,21 +354,21 @@
         for i in range(len(regions[1 - f])):
             spread(1 - f, i, side, near_sems, beside).wait_recv()
             write(1 - f, i, side, 2).start()
-        for i in range(len(regions[1 - f])):
-            spread(1 - f, i, 1 - side, last_sems, beside).wait_recv()
-            write(1 - f, i, 1 - side, 3).start()
-        for i in range(len(regions[f])):
-            write(f, i, side, 0).wait()
-            write(f, i, 1 - side, 1).wait()
-        for i in range(len(regions[1 - f])):
-            write(1 - f, i, side, 2).wait()
-            write(1 - f, i, 1 - side, 3).wait()
         for a in range(bands if f == 0 else len(shared)):
             swap(f, a).wait_send()
         for i in range(len(regions[f])):
             spread(f, i, side, far_sems, across).wait_send()
             spread(f, i, side, near_sems, beside).wait_send()
+            write(f, i, side, 0).wait()
+        for i in range(len(regions[1 - f])):
+            spread(1 - f, i, 1 - side, last_sems, beside).wait_recv()
+            write(1 - f, i, 1 - side, 3).start()
+        for i in range(len(regions[f])):
             spread(f, i, 1 - side, last_sems, beside).wait_send()
+            write(f, i, 1 - side, 1).wait()
+        for i in range(len(regions[1 - f])):
+            write(1 - f, i, side, 2).wait()
+            write(1 - f, i, 1 - side, 3).wait()
 
     progress = {"arrived": 0, "band": 0}
 
@@ -409,8 +409,6 @@
 
     lax.fori_loop(0, K + AHEAD, step, 0)
     ready(K - 1)
-    for f in range(2):
-        pl.when(flip == f)(functools.partial(settle, f))
 
     def drain(k, carry):
         for r in range(1, U):
@@ -428,6 +426,8 @@
     lax.fori_loop(0, K, drain, 0)
     for copy in em_sends:
         copy.wait_send()
+    for f in range(2):
+        pl.when(flip == f)(functools.partial(settle, f))
 
 
 def on_device(atten, view_segment, efficiency, live_mask):
@@ -447,9 +447,9 @@
     far = pl.BlockSpec(memory_space=pl.ANY)
     out = pl.pallas_call(
         functools.partial(kernel, dims),
-        out_shape=jax.ShapeDtypeStruct((2 * half, D, square), f32),
+        out_shape=pltpu.VMEM((2 * half, D, square), f32),
         in_specs=[pl.BlockSpec(memory_space=pltpu.SMEM), far, far, far],
-        out_specs=far,
+        out_specs=pl.BlockSpec(memory_space=pltpu.VMEM),
         scratch_shapes=[
             pltpu.VMEM((D, N, N), f32),
             pltpu.VMEM((2, 2, K, CHUNK, R), f32),
@@ -472,7 +472,7 @@
             dma((K,)), dma((K,)), dma((K, G)), dma((K, G)),
             dma((square // LANES,)), dma((square // LANES,)), *[dma((3,))] * 6, dma((4, 3)),
         ],
-        compiler_params=pltpu.CompilerParams(collective_id=0, has_side_effects=True, vmem_limit_bytes=63 * 2**20),
+        compiler_params=pltpu.CompilerParams(collective_id=0, has_side_effects=True, vmem_limit_bytes=61 * 2**20),
     )(view_segment, jnp.transpose(atten, (1, 0, 2)), jnp.transpose(efficiency, (2, 0, 1)), jnp.transpose(live_mask, (2, 0, 1)))
     return jnp.transpose(out[:N, :, :N], (1, 0, 2))
 

time: 46.7 us -> 44.7 us (0.957)
  local copies, waits for them, and re-layouts: 2.58 us -> 1.35 us
  Pallas kernels: 44 us -> 43.2 us
    transpose x1, local copies, waits for them, and re-layouts: 2.58 us -> 1.35 us  [on_device(): return jnp.transpose(out[:N, :, :N], (1, 0, 2))]
    pallas_call x1, Pallas kernels: 44 us -> 43.2 us  [on_device(): pl.pallas_call(functools.partial(kernel, dims), out_shape=pltpu.VMEM((2 *...]
where the time goes in v7:
time: 44.7 us; the launch traced here: 44.6 us
  Pallas kernels  43.2 us (97%)
  local copies, waits for them, and re-layouts  1.35 us (3%)
    pallas_call x1, Pallas kernels, on_device(): pl.pallas_call(functools.partial(kernel, dims), out_shape=pltpu.VMEM((2 *...  43.2 us
    transpose x1, local copies, waits for them, and re-layouts, on_device(): return jnp.transpose(out[:N, :, :N], (1, 0, 2))  1.35 us

profile of v7, /device:TPU:0, one launch (start us, length us, event | category | flops | bytes accessed | tf_op | source)
XLA Modules:
  0.0 44.6 jit_solution(8094313556291360380)
XLA Ops:
  0.0 43.2 %shard_map.46 = f32[352,2,384]{2,1,0:T(2,128)S(1)} custom-call(s32[2]{0:T(128)} %seg_ref.1, f32[350,2,350]{2,1,0:T(2,128)} %bitcast.5, f32[350,2,376]{2,1,0:T(2,128)} %bitcast.6, s32[350,2,376]{2,1,0:T(2,128)} %bitcast.7), custom_call_target="tpu_custom_call" | custom-call | tf_op jit(solution)/shard_map/pallas_call | solution.py:448
  43.2 1.3 %slice_bitcast_fusion = f32[2,350,350]{2,0,1:T(2,128)} fusion(f32[352,2,384]{2,1,0:T(2,128)S(1)} %shard_map.46), kind=kLoop, calls=%fused_computation | loop fusion | bytes 1960000 | tf_op jit(solution)/shard_map/transpose | solution.py:477

commit v8 on v7

--- a/solution.py
+++ b/solution.py
@@ -11,8 +11,8 @@
 NSEG = 4
 TILE = 8
 LANES = 128
-CHUNK = 8
-AHEAD = 2
+CHUNK = 16
+AHEAD = 1
 
 
 def round_up(value, unit):

time: 44.7 us -> 44.7 us (level)
  no operation moved by 1% of the time
where the time goes in v8:
time: 44.7 us; the launch traced here: 44.5 us
  Pallas kernels  43.1 us (96%)
  local copies, waits for them, and re-layouts  1.35 us (3%)
    pallas_call x1, Pallas kernels, on_device(): pl.pallas_call(functools.partial(kernel, dims), out_shape=pltpu.VMEM((2 *...  43.1 us
    transpose x1, local copies, waits for them, and re-layouts, on_device(): return jnp.transpose(out[:N, :, :N], (1, 0, 2))  1.35 us

profile of v8, /device:TPU:0, one launch (start us, length us, event | category | flops | bytes accessed | tf_op | source)
XLA Modules:
  0.0 44.5 jit_solution(10293370196888707871)
XLA Ops:
  0.0 43.1 %shard_map.46 = f32[352,2,384]{2,1,0:T(2,128)S(1)} custom-call(s32[2]{0:T(128)} %seg_ref.1, f32[350,2,350]{2,1,0:T(2,128)} %bitcast.5, f32[350,2,376]{2,1,0:T(2,128)} %bitcast.6, s32[350,2,376]{2,1,0:T(2,128)} %bitcast.7), custom_call_target="tpu_custom_call" | custom-call | tf_op jit(solution)/shard_map/pallas_call | solution.py:448
  43.2 1.3 %slice_bitcast_fusion = f32[2,350,350]{2,0,1:T(2,128)} fusion(f32[352,2,384]{2,1,0:T(2,128)S(1)} %shard_map.46), kind=kLoop, calls=%fused_computation | loop fusion | bytes 1960000 | tf_op jit(solution)/shard_map/transpose | solution.py:477

commit v9 on v8

--- a/solution.py
+++ b/solution.py
@@ -151,7 +151,7 @@
 
         while started < K and ((started + 1) * G * CHUNK <= b + LANES or b + LANES == square):
             k = started
-            for r in range(1, U):
+            for r in [*range(U // 2, U), *range(1, U // 2)]:
                 g, copy = outgoing(k, r)
                 guarded(k, g, copy.start)
 
@@ -270,7 +270,7 @@
         image[rows_of(k, me), :] = back[k, unit, side]
 
     def returning(k):
-        for r in range(U):
+        for r in [*range(U // 2, U), *range(U // 2)]:
             to_unit = lax.rem(unit + r, U)
             for e in range(2):
                 if r or e:

time: 44.7 us -> 44.8 us (level)
  no operation moved by 1% of the time
where the time goes in v9:
time: 44.8 us; the launch traced here: 44.6 us
  Pallas kernels  43.3 us (97%)
  local copies, waits for them, and re-layouts  1.35 us (3%)
    pallas_call x1, Pallas kernels, on_device(): pl.pallas_call(functools.partial(kernel, dims), out_shape=pltpu.VMEM((2 *...  43.3 us
    transpose x1, local copies, waits for them, and re-layouts, on_device(): return jnp.transpose(out[:N, :, :N], (1, 0, 2))  1.35 us

profile of v9, /device:TPU:0, one launch (start us, length us, event | category | flops | bytes accessed | tf_op | source)
XLA Modules:
  0.0 44.6 jit_solution(8582556339365315707)
XLA Ops:
  0.0 43.3 %shard_map.46 = f32[352,2,384]{2,1,0:T(2,128)S(1)} custom-call(s32[2]{0:T(128)} %seg_ref.1, f32[350,2,350]{2,1,0:T(2,128)} %bitcast.5, f32[350,2,376]{2,1,0:T(2,128)} %bitcast.6, s32[350,2,376]{2,1,0:T(2,128)} %bitcast.7), custom_call_target="tpu_custom_call" | custom-call | tf_op jit(solution)/shard_map/pallas_call | solution.py:448
  43.3 1.3 %slice_bitcast_fusion = f32[2,350,350]{2,0,1:T(2,128)} fusion(f32[352,2,384]{2,1,0:T(2,128)S(1)} %shard_map.46), kind=kLoop, calls=%fused_computation | loop fusion | bytes 1960000 | tf_op jit(solution)/shard_map/transpose | solution.py:477
